TPU v7x, 32 devices: a whole 2x2x4 slice. The times are simulated.
32 devices in a mesh: dp: 4 (over y, x), ctx: 8 (over z, core).
Axes of the slice: x: 2, y: 2, z: 4, core: 2. Of those that a mesh axis runs over, the one named last changes fastest.
Arguments:
- layer_input: bfloat16 [4, 1024, 2048], P('dp', 'ctx'), may hold values from -6 to 6
- prefix: int32 [4], P('dp'), may hold values from 102 to 512
- wq: bfloat16 [2048, 2048], P(('dp', 'ctx')), may hold values from -0.125 to 0.125
- wk: bfloat16 [2048, 1024], P(('dp', 'ctx')), may hold values from -0.125 to 0.125
- wv: bfloat16 [2048, 1024], P(('dp', 'ctx')), may hold values from -0.125 to 0.125
- wo: bfloat16 [2048, 2048], P(('dp', 'ctx')), may hold values from -2 to 2
- w_gate: bfloat16 [2048, 6144], P(('dp', 'ctx')), may hold values from -0.125 to 0.125
- w_up: bfloat16 [2048, 6144], P(('dp', 'ctx')), may hold values from -0.125 to 0.125
- w_down: bfloat16 [6144, 2048], P(('dp', 'ctx')), may hold values from -0.078125 to 0.078125
- gains: bfloat16 [4352], P(('dp', 'ctx')), may hold values from 0.5 to 1.5
- cotangent: bfloat16 [4, 1024, 2048], P('dp', 'ctx'), may hold values from -6 to 6
Outputs:
- layer_output: bfloat16 [4, 1024, 2048], P('dp', 'ctx')
- x_grad: bfloat16 [4, 1024, 2048], P('dp', 'ctx')
- wq_grad: float32 [2048, 2048], P(('dp', 'ctx'))
- wk_grad: float32 [2048, 1024], P(('dp', 'ctx'))
- wv_grad: float32 [2048, 1024], P(('dp', 'ctx'))
- wo_grad: float32 [2048, 2048], P(('dp', 'ctx'))
- gate_grad: float32 [2048, 6144], P(('dp', 'ctx'))
- up_grad: float32 [2048, 6144], P(('dp', 'ctx'))
- down_grad: float32 [6144, 2048], P(('dp', 'ctx'))
- gains_grad: float32 [4352], P(('dp', 'ctx'))
Inputs may be any that keep to these rules, and one draw needn't show every extreme that they name: prefix[s] keys at the start of sequence s are seen by every query of that sequence.
All inputs are finite; a program needn't handle non-finite values.
Results may differ from a plain program's by a relative error of at most 0.015.
Values may be sent and summed in bfloat16 or wider, within the bound.
A program may use at most 512 MiB of HBM per device.

v0:
```python
import jax
import jax.numpy as jnp
from jax import lax
from jax.sharding import PartitionSpec as P

MODEL_WIDTH = 2048
QUERY_HEADS = 16
KEY_VALUE_HEADS = 8
HEAD_SIZE = 128


EPSILON = 1e-06
ROPE_BASE = 1000000.0


def rms_scale(value, gain):
    return value * lax.rsqrt(jnp.mean(value * value, -1, keepdims=True) + EPSILON) * gain


def rotate(value, cosine, sine):
    half = value.shape[-1] // 2
    first = value[..., :half]
    second = value[..., half:]
    return jnp.concatenate([first * cosine - second * sine, second * cosine + first * sine], -1)


def matrix_product(left, right):
    return jnp.dot(left, right, preferred_element_type=jnp.float32)


def inner_rows(left, right):
    return lax.dot_general(
        left, right, (((0,), (0,)), ((), ())), preferred_element_type=jnp.float32
    )


def outer_columns(left, right):
    return lax.dot_general(
        left, right, (((1,), (1,)), ((), ())), preferred_element_type=jnp.float32
    )


def gated_unit(gate, up):
    return jax.nn.silu(gate) * up


def shards(layer_input, prefix, wq, wk, wv, wo, w_gate, w_up, w_down, gains, cotangent):
    attn_set = (
        lax.all_gather(wq, ("dp", "ctx"), axis=0, tiled=True),
        lax.all_gather(wk, ("dp", "ctx"), axis=0, tiled=True),
        lax.all_gather(wv, ("dp", "ctx"), axis=0, tiled=True),
        lax.all_gather(wo, ("dp", "ctx"), axis=0, tiled=True),
        lax.all_gather(gains, ("dp", "ctx"), axis=0, tiled=True),
    )
    mlp_set = (
        lax.all_gather(w_gate, ("dp", "ctx"), axis=0, tiled=True),
        lax.all_gather(w_up, ("dp", "ctx"), axis=0, tiled=True),
        lax.all_gather(w_down, ("dp", "ctx"), axis=0, tiled=True),
    )
    full_q, complete_key_weight, full_v, complete_output_weight, full_gains = attn_set
    full_gate, full_up, full_down = mlp_set
    token_rows = layer_input.shape[1]
    sequence_length = token_rows * lax.axis_size("ctx")
    query_group_size = QUERY_HEADS // KEY_VALUE_HEADS
    key_value_width = KEY_VALUE_HEADS * HEAD_SIZE
    scale = HEAD_SIZE ** (-0.5)
    gain_all = full_gains.astype(jnp.float32)
    gain_one = gain_all[:MODEL_WIDTH]
    gain_two = gain_all[MODEL_WIDTH : 2 * MODEL_WIDTH]
    gain_q = gain_all[2 * MODEL_WIDTH : 2 * MODEL_WIDTH + HEAD_SIZE]
    gain_k = gain_all[2 * MODEL_WIDTH + HEAD_SIZE :]
    qpos = lax.axis_index("ctx") * token_rows + jnp.arange(token_rows, dtype=jnp.int32)
    kpos = jnp.arange(sequence_length, dtype=jnp.int32)
    visible = (kpos[None, :] <= qpos[:, None]) | (kpos[None, :] < prefix[0])
    freqs = ROPE_BASE ** (-(jnp.arange(HEAD_SIZE // 2, dtype=jnp.float32) * 2.0 / HEAD_SIZE))
    angles = qpos.astype(jnp.float32)[:, None] * freqs[None, :]
    cosine = jnp.cos(angles)[:, None, :]
    sine = jnp.sin(angles)[:, None, :]

    def prepare_heads(raw, gain):
        return rotate(rms_scale(raw, gain), cosine, sine)

    def head_scores(q_one, k_one):
        raw = jnp.einsum("tgd,sd->gts", q_one, k_one, preferred_element_type=jnp.float32) * scale
        return jnp.where(visible[None], raw, -1e30)

    def attend_head(item):
        q_one, k_one, v_one = item
        scores = head_scores(q_one, k_one)
        top = jnp.max(scores, -1, keepdims=True)
        expo = jnp.exp(scores - top)
        total = jnp.sum(expo, -1, keepdims=True)
        probs_bf = (expo / total).astype(jnp.bfloat16)
        result = jnp.einsum("gts,sd->tgd", probs_bf, v_one, preferred_element_type=jnp.float32)
        return (result, top + jnp.log(total))

    def attend_back(item):
        q_one, k_one, v_one, d_one, lse_one = item
        probs = jnp.exp(head_scores(q_one, k_one) - lse_one)
        probs_bf = probs.astype(jnp.bfloat16)
        d_probs = jnp.einsum("tgd,sd->gts", d_one, v_one, preferred_element_type=jnp.float32)
        value_part = jnp.einsum("gts,tgd->sd", probs_bf, d_one, preferred_element_type=jnp.float32)
        d_scores = probs * (d_probs - jnp.sum(d_probs * probs, -1, keepdims=True))
        d_scores = d_scores.astype(jnp.bfloat16)
        d_query = (
            jnp.einsum("gts,sd->tgd", d_scores, k_one, preferred_element_type=jnp.float32) * scale
        )
        key_part = (
            jnp.einsum("gts,tgd->sd", d_scores, q_one, preferred_element_type=jnp.float32) * scale
        )
        return (d_query, key_part, value_part)

    inputs = layer_input[0].astype(jnp.float32)
    first_normalized, back_one = jax.vjp(rms_scale, inputs, gain_one)
    first_normalized = first_normalized.astype(jnp.bfloat16)
    q_raw = matrix_product(first_normalized, full_q).reshape(token_rows, QUERY_HEADS, HEAD_SIZE)
    unrotated_keys = matrix_product(first_normalized, complete_key_weight).reshape(
        token_rows, KEY_VALUE_HEADS, HEAD_SIZE
    )
    v_local = matrix_product(first_normalized, full_v).astype(jnp.bfloat16)
    rotated_queries, back_q = jax.vjp(prepare_heads, q_raw, gain_q)
    k_rot, back_k = jax.vjp(prepare_heads, unrotated_keys, gain_k)
    query_head_rows = jnp.transpose(
        rotated_queries.astype(jnp.bfloat16).reshape(
            token_rows, KEY_VALUE_HEADS, query_group_size, HEAD_SIZE
        ),
        (1, 0, 2, 3),
    )
    k_local = k_rot.astype(jnp.bfloat16).reshape(token_rows, key_value_width)
    every_key_row, every_value_row = (
        lax.all_gather(k_local, "ctx", axis=0, tiled=True),
        lax.all_gather(v_local, "ctx", axis=0, tiled=True),
    )
    key_head_rows = jnp.transpose(
        every_key_row.reshape(sequence_length, KEY_VALUE_HEADS, HEAD_SIZE), (1, 0, 2)
    )
    value_head_rows = jnp.transpose(
        every_value_row.reshape(sequence_length, KEY_VALUE_HEADS, HEAD_SIZE), (1, 0, 2)
    )
    attended, lse = lax.map(attend_head, (query_head_rows, key_head_rows, value_head_rows))
    attended = (
        jnp.transpose(attended, (1, 0, 2, 3))
        .reshape(token_rows, QUERY_HEADS * HEAD_SIZE)
        .astype(jnp.bfloat16)
    )
    hidden = inputs + matrix_product(attended, complete_output_weight)
    normed_two, back_two = jax.vjp(rms_scale, hidden, gain_two)
    normed_two = normed_two.astype(jnp.bfloat16)
    gate = matrix_product(normed_two, full_gate)
    up = matrix_product(normed_two, full_up)
    active, back_gated = jax.vjp(gated_unit, gate, up)
    active = active.astype(jnp.bfloat16)
    output = (hidden + matrix_product(active, full_down)).astype(jnp.bfloat16)
    mlp_set = (
        lax.all_gather(w_gate, ("dp", "ctx"), axis=0, tiled=True),
        lax.all_gather(w_up, ("dp", "ctx"), axis=0, tiled=True),
        lax.all_gather(w_down, ("dp", "ctx"), axis=0, tiled=True),
    )
    attn_set = (
        lax.all_gather(wq, ("dp", "ctx"), axis=0, tiled=True),
        lax.all_gather(wk, ("dp", "ctx"), axis=0, tiled=True),
        lax.all_gather(wv, ("dp", "ctx"), axis=0, tiled=True),
        lax.all_gather(wo, ("dp", "ctx"), axis=0, tiled=True),
        lax.all_gather(gains, ("dp", "ctx"), axis=0, tiled=True),
    )
    full_gate, full_up, full_down = mlp_set
    full_q, complete_key_weight, full_v, complete_output_weight, full_gains = attn_set
    upstream = cotangent[0].astype(jnp.float32)
    upstream_bf = upstream.astype(jnp.bfloat16)
    down_term = inner_rows(active, upstream_bf)
    down_grad = lax.psum_scatter(down_term, ("dp", "ctx"), scatter_dimension=0, tiled=True)
    d_active = outer_columns(upstream_bf, full_down)
    d_gate, d_up = back_gated(d_active)
    d_gate = d_gate.astype(jnp.bfloat16)
    d_up = d_up.astype(jnp.bfloat16)
    gate_term = inner_rows(normed_two, d_gate)
    up_term = inner_rows(normed_two, d_up)
    gate_grad, up_grad = (
        lax.psum_scatter(gate_term, ("dp", "ctx"), scatter_dimension=0, tiled=True),
        lax.psum_scatter(up_term, ("dp", "ctx"), scatter_dimension=0, tiled=True),
    )
    d_normed_two = outer_columns(d_gate, full_gate) + outer_columns(d_up, full_up)
    d_hidden_part, d_gain_two = back_two(d_normed_two)
    d_hidden = upstream + d_hidden_part
    attention_gradient = d_hidden.astype(jnp.bfloat16)
    out_term = inner_rows(attended, attention_gradient)
    output_gradient = (
        outer_columns(attention_gradient, complete_output_weight)
        .astype(jnp.bfloat16)
        .reshape(token_rows, KEY_VALUE_HEADS, query_group_size, HEAD_SIZE)
    )
    d_out_heads = jnp.transpose(output_gradient, (1, 0, 2, 3))
    d_q_heads, key_term, value_term = lax.map(
        attend_back, (query_head_rows, key_head_rows, value_head_rows, d_out_heads, lse)
    )
    d_q_rot = jnp.transpose(d_q_heads, (1, 0, 2, 3))
    key_term = jnp.transpose(key_term, (1, 0, 2)).reshape(sequence_length, key_value_width)
    value_term = jnp.transpose(value_term, (1, 0, 2)).reshape(sequence_length, key_value_width)
    kv_term = jnp.concatenate([key_term, value_term], 1)
    key_value_gradient = lax.psum_scatter(kv_term, "ctx", scatter_dimension=0, tiled=True)
    rotated_key_gradient = key_value_gradient[:, :key_value_width].reshape(
        token_rows, KEY_VALUE_HEADS, HEAD_SIZE
    )
    d_values = key_value_gradient[:, key_value_width:].astype(jnp.bfloat16)
    d_q_raw, d_gain_q = back_q(d_q_rot.reshape(token_rows, QUERY_HEADS, HEAD_SIZE))
    d_k_raw, d_gain_k = back_k(rotated_key_gradient)
    d_queries = d_q_raw.reshape(token_rows, QUERY_HEADS * HEAD_SIZE).astype(jnp.bfloat16)
    d_keys = d_k_raw.reshape(token_rows, key_value_width).astype(jnp.bfloat16)
    query_term = inner_rows(first_normalized, d_queries)
    keyw_term = inner_rows(first_normalized, d_keys)
    valuew_term = inner_rows(first_normalized, d_values)
    d_normed_one = (
        outer_columns(d_queries, full_q)
        + outer_columns(d_keys, complete_key_weight)
        + outer_columns(d_values, full_v)
    )
    d_input_part, d_gain_one = back_one(d_normed_one)
    input_grad = (d_hidden + d_input_part).astype(jnp.bfloat16)
    gain_term = jnp.concatenate([d_gain_one, d_gain_two, d_gain_q, d_gain_k])
    wq_grad, wk_grad, wv_grad, wo_grad, gains_grad = (
        lax.psum_scatter(query_term, ("dp", "ctx"), scatter_dimension=0, tiled=True),
        lax.psum_scatter(keyw_term, ("dp", "ctx"), scatter_dimension=0, tiled=True),
        lax.psum_scatter(valuew_term, ("dp", "ctx"), scatter_dimension=0, tiled=True),
        lax.psum_scatter(out_term, ("dp", "ctx"), scatter_dimension=0, tiled=True),
        lax.psum_scatter(gain_term, ("dp", "ctx"), scatter_dimension=0, tiled=True),
    )
    return (
        output[None],
        input_grad[None],
        wq_grad,
        wk_grad,
        wv_grad,
        wo_grad,
        gate_grad,
        up_grad,
        down_grad,
        gains_grad,
    )


def solution(mesh):
    return jax.shard_map(
        shards,
        mesh=mesh,
        in_specs=(
            P("dp", "ctx", None),
            P("dp"),
            P(("dp", "ctx"), None),
            P(("dp", "ctx"), None),
            P(("dp", "ctx"), None),
            P(("dp", "ctx"), None),
            P(("dp", "ctx"), None),
            P(("dp", "ctx"), None),
            P(("dp", "ctx"), None),
            P(("dp", "ctx")),
            P("dp", "ctx", None),
        ),
        out_specs=(
            P("dp", "ctx", None),
            P("dp", "ctx", None),
            P(("dp", "ctx"), None),
            P(("dp", "ctx"), None),
            P(("dp", "ctx"), None),
            P(("dp", "ctx"), None),
            P(("dp", "ctx"), None),
            P(("dp", "ctx"), None),
            P(("dp", "ctx"), None),
            P(("dp", "ctx")),
        ),
        check_vma=False,
    )
```

profile of v0, /device:TPU:1, one launch (start us, length us, event | category | flops | bytes accessed | tf_op | source)
XLA Modules:
  0.0 3052.3 jit_solution(10670143161202191854)
XLA Ops:
  9.6 42.0 %all-reduce.4 = bf16[4352]{0:T(1024)(128)(2,1)S(1)} all-reduce(bf16[4352]{0:T(1024)(128)(2,1)S(1)} %dynamic-update-slice), channel_id=1, replica_groups=mesh['dp'=4,'ctx'=8] {'dp','ctx'}, use_global_device_ids=true, to_apply=%add.4 | all-reduce | flops 4352 | bytes 17408
  53.5 22.2 all-gather.14.cloned.1.call-done
  75.8 6.6 copy.49
  82.4 3.5 multiply_reduce_fusion.9
  87.7 51.8 %all-gather.10.cloned.1.call-done = bf16[2048,1024]{1,0:T(8,128)(2,1)} async-done(((bf16[64,1024]{1,0:T(8,128)(2,1)}), bf16[2048,1024]{1,0:T(8,128)(2,1)}) %all-gather.10.cloned.1.call-update) | async-done | bytes 4194320 | tf_op jit(solution)/shard_map/all_gather | solution.py:51
  139.5 3.7 convolution_convert_fusion.1
  147.4 23.6 all-gather.16.cloned.1.call-done
  171.1 3.0 copy.54
  174.1 27.2 all-gather.12.cloned.1.call-done
  201.3 3.6 copy.85
  204.9 4.2 copy.53
  209.0 3.3 bitcast_bitcast_fusion
  212.3 68.7 %all-gather.18.cloned.1.call-done = bf16[2048,2048]{1,0:T(8,128)(2,1)} async-done(((bf16[64,2048]{1,0:T(8,128)(2,1)}), bf16[2048,2048]{1,0:T(8,128)(2,1)}) %all-gather.18.cloned.1.call-update) | async-done | bytes 8388624 | tf_op jit(solution)/shard_map/all_gather | solution.py:49
  281.1 12.4 copy.50
  293.4 5.9 multiply_reduce_fusion.6
  301.4 2.0 copy.51
  304.4 2.3 maximum_bitcast_fusion
  306.6 23.5 while.30
  330.2 29.8 all-gather.20.cloned.1.call-done
  360.0 4.7 multiply_reduce_fusion.5
  364.9 151.4 %all-gather.22.cloned.1.call-done = bf16[2048,6144]{1,0:T(8,128)(2,1)} async-done(((bf16[64,6144]{1,0:T(8,128)(2,1)}), bf16[2048,6144]{1,0:T(8,128)(2,1)}) %all-gather.22.cloned.1.call-update) | async-done | bytes 25165840 | tf_op jit(solution)/shard_map/all_gather | solution.py:56
  516.3 13.2 fusion.104
  529.5 142.7 %all-gather.24.cloned.1.call-done = bf16[2048,6144]{1,0:T(8,128)(2,1)} async-done(((bf16[64,6144]{1,0:T(8,128)(2,1)}), bf16[2048,6144]{1,0:T(8,128)(2,1)}) %all-gather.24.cloned.1.call-update) | async-done | bytes 25165840 | tf_op jit(solution)/shard_map/all_gather | solution.py:57
  672.2 13.2 fusion.105
  685.5 142.7 %all-gather.26.cloned.1.call-done = bf16[6144,2048]{1,0:T(8,128)(2,1)} async-done(((bf16[192,2048]{1,0:T(8,128)(2,1)}), bf16[6144,2048]{1,0:T(8,128)(2,1)}) %all-gather.26.cloned.1.call-update) | async-done | bytes 25165840 | tf_op jit(solution)/shard_map/all_gather | solution.py:58
  828.1 16.4 multiply_convert_fusion.1
  844.6 14.6 fusion.106
  859.2 14.6 multiply_reduce_fusion.2
  875.1 6.3 convolution_convert_fusion
  882.7 72.2 %while.31 = (s32[]{:T(128)}, f32[8,128,2,128]{1,3,2,0:T(8,128)}, f32[8,1024,128]{1,2,0:T(8,128)}, f32[8,1024,128]{1,2,0:T(8,128)}, bf16[8,1024,128]{2,1,0:T(8,12...) while((s32[]{:T(128)}, f32[8,128,2,128]{1,3,2,0:T(8,128)}, ...), condition=%wide.region_11.12_spmd.clone.clone, body=%wide.region_9.11_spmd.clone.sunk.clone | while | flops 338329344 | bytes 12463729 | solution.py:193
  887.9 1.9 fusion.199
  889.8 1.9 fusion.197
  896.9 2.0 fusion.199
  898.9 1.9 fusion.197
  906.0 2.0 fusion.199
  907.9 1.9 fusion.197
  915.0 1.9 fusion.199
  916.9 1.9 fusion.197
  924.0 1.9 fusion.199
  925.9 1.9 fusion.197
  933.0 1.9 fusion.199
  934.9 1.9 fusion.197
  942.0 2.0 fusion.199
  944.0 1.9 fusion.197
  951.1 1.9 fusion.199
  953.0 1.9 fusion.197
  954.9 8.3 pad_maximum_fusion
  963.5 85.1 %reduce-scatter.9.cloned.1.call-done = f32[128,2048]{0,1:T(8,128)} async-done(((f32[1024,2048]{0,1:T(8,128)}), f32[128,2048]{0,1:T(8,128)}) %reduce-scatter.9.cloned.1.call-update) | async-done | bytes 1048592 | tf_op jit(solution)/shard_map/reduce_scatter | solution.py:200
  1050.1 4.6 fusion.82
  1056.1 8.1 fusion.86
  1065.4 4.7 fusion.89
  1072.4 8.2 fusion.84
  1081.6 21.2 fusion.108
  1102.9 21.2 fusion.109
  1125.1 21.1 fusion.74
  1146.2 6.5 fusion.107
  1152.8 11.2 fusion.55
  1168.3 40.6 %all-reduce.5 = f32[4352]{0:T(1024)S(1)} all-reduce(f32[4352]{0:T(1024)S(1)} %pad_maximum_fusion.2), channel_id=10, replica_groups=mesh['dp'=4,'ctx'=8] {'dp','ctx'}, use_global_device_ids=true, to_apply=%region_27.28.clone | all-reduce | flops 4352 | bytes 34816
  1210.7 180.0 %reduce-scatter.17.cloned.1.call-done = f32[64,2048]{1,0:T(8,128)} async-done(((f32[2048,2048]{1,0:T(8,128)}), f32[64,2048]{1,0:T(8,128)}) %reduce-scatter.17.cloned.1.call-update) | async-done | bytes 524304 | tf_op jit(solution)/shard_map/reduce_scatter | solution.py:224
  1390.7 152.7 %reduce-scatter.15.cloned.1.call-done = f32[64,1024]{1,0:T(8,128)} async-done(((f32[2048,1024]{1,0:T(8,128)}), f32[64,1024]{1,0:T(8,128)}) %reduce-scatter.15.cloned.1.call-update) | async-done | bytes 262160 | tf_op jit(solution)/shard_map/reduce_scatter | solution.py:223
  1543.5 186.9 %reduce-scatter.11.cloned.1.call-done = f32[64,2048]{1,0:T(8,128)} async-done(((f32[2048,2048]{1,0:T(8,128)}), f32[64,2048]{1,0:T(8,128)}) %reduce-scatter.11.cloned.1.call-update) | async-done | bytes 524304 | tf_op jit(solution)/shard_map/reduce_scatter | solution.py:221
  1730.4 440.1 %reduce-scatter.19.cloned.1.call-done = f32[64,6144]{1,0:T(8,128)} async-done(((f32[2048,6144]{1,0:T(8,128)}), f32[64,6144]{1,0:T(8,128)}) %reduce-scatter.19.cloned.1.call-update) | async-done | bytes 1572880 | tf_op jit(solution)/shard_map/reduce_scatter | solution.py:179
  2170.5 437.4 %reduce-scatter.21.cloned.1.call-done = f32[64,6144]{1,0:T(8,128)} async-done(((f32[2048,6144]{1,0:T(8,128)}), f32[64,6144]{1,0:T(8,128)}) %reduce-scatter.21.cloned.1.call-update) | async-done | bytes 1572880 | tf_op jit(solution)/shard_map/reduce_scatter | solution.py:180
  2607.9 437.5 %reduce-scatter.23.cloned.1.call-done = f32[192,2048]{1,0:T(8,128)} async-done(((f32[6144,2048]{1,0:T(8,128)}), f32[192,2048]{1,0:T(8,128)}) %reduce-scatter.23.cloned.1.call-update) | async-done | bytes 1572880 | tf_op jit(solution)/shard_map/reduce_scatter | solution.py:171
  (234 shorter events, 94.4 us)
Async XLA Ops:
  7.2 68.6 %all-gather.14.cloned.1.call-start = ((), (), s32[]{:S(2)}) async-start(), calls=%async_computation.10 | async-start | bytes 4325376 | tf_op jit(solution)/shard_map/all_gather | solution.py:50
  7.9 131.6 %all-gather.10.cloned.1.call-start = ((), (), s32[]{:S(2)}) async-start(), calls=%async_computation.8 | async-start | bytes 4325376 | tf_op jit(solution)/shard_map/all_gather | solution.py:51
  8.7 162.4 %all-gather.16.cloned.1.call-start = ((), (), s32[]{:S(2)}) async-start(), calls=%async_computation.11 | async-start | bytes 2359296 | tf_op jit(solution)/shard_map/all_gather | solution.py:131
  52.8 0.5 copy-start.23
  75.8 6.6 copy-start
  85.9 0.8 copy-start.14
  87.6 113.6 %all-gather.12.cloned.1.call-start = ((), (), s32[]{:S(2)}) async-start(), calls=%async_computation.9 | async-start | bytes 2359296 | tf_op jit(solution)/shard_map/all_gather | solution.py:132
  143.2 137.9 %all-gather.18.cloned.1.call-start = ((), (), s32[]{:S(2)}) async-start(), calls=%async_computation.12 | async-start | bytes 8650752 | tf_op jit(solution)/shard_map/all_gather | solution.py:49
  143.8 216.2 %all-gather.20.cloned.1.call-start = ((), (), s32[]{:S(2)}) async-start(), calls=%async_computation.13 | async-start | bytes 8650752 | tf_op jit(solution)/shard_map/all_gather | solution.py:52
  144.3 372.0 %all-gather.22.cloned.1.call-start = ((), (), s32[]{:S(2)}) async-start(), calls=%async_computation.14 | async-start | bytes 25952256 | tf_op jit(solution)/shard_map/all_gather | solution.py:56
  145.1 527.1 %all-gather.24.cloned.1.call-start = ((), (), s32[]{:S(2)}) async-start(), calls=%async_computation.15 | async-start | bytes 25952256 | tf_op jit(solution)/shard_map/all_gather | solution.py:57
  145.8 682.3 %all-gather.26.cloned.1.call-start = ((), (), s32[]{:S(2)}) async-start(), calls=%async_computation.16 | async-start | bytes 25952256 | tf_op jit(solution)/shard_map/all_gather | solution.py:58
  146.6 902.1 %reduce-scatter.9.cloned.1.call-start = ((), (), s32[]{:S(2)}) async-start(), calls=%async_computation.17 | async-start | bytes 9437184 | tf_op jit(solution)/shard_map/reduce_scatter | solution.py:200
  299.3 1.0 copy-start.3
  330.2 29.8 copy-start.12
  330.2 34.5 %copy-start.16 = (bf16[8,128,2,128]{1,3,2,0:T(8,128)(2,1)}, bf16[8,128,2,128]{1,3,2,0:T(8,128)(2,1)S(1)}, u32[]{:S(2)}) copy-start(bf16[8,128,2,128]{1,3,2,0:T(8,128)(2,1)S(1)} %get-tuple-element.102) | copy-start | bytes 1572868
  364.7 509.1 %copy-start.1 = (f32[128,2048]{1,0:T(8,128)}, f32[128,2048]{1,0:T(8,128)S(1)}, u32[]{:S(2)}) copy-start(f32[128,2048]{1,0:T(8,128)S(1)} %get-tuple-element.271) | copy-start | bytes 3145732
  364.9 307.3 %copy-start.9 = (bf16[128,2048]{1,0:T(8,128)(2,1)}, bf16[128,2048]{1,0:T(8,128)(2,1)S(1)}, u32[]{:S(2)}) copy-start(bf16[128,2048]{1,0:T(8,128)(2,1)S(1)} %multiply_convert_fusion.3) | copy-start | bytes 1572868
  844.6 14.6 copy-start.11
  859.2 14.6 copy-start.20
  874.1 1.0 copy-start.6
  963.2 86.6 %copy-start.15 = (f32[128,8,128]{0,2,1:T(8,128)S(1)}, f32[128,8,128]{0,2,1:T(8,128)}, u32[]{:S(2)}) copy-start(f32[128,8,128]{0,2,1:T(8,128)} %copy-done.14) | copy-start | bytes 1572868
  963.3 247.5 %reduce-scatter.13.cloned.1.call-start = ((), (), s32[]{:S(2)}) async-start(), calls=%async_computation.19 | async-start | bytes 8650752 | tf_op jit(solution)/shard_map/reduce_scatter | solution.py:222
  1054.7 1.2 copy-start.7
  1054.7 1.4 copy-start.17
  1054.8 336.0 %reduce-scatter.17.cloned.1.call-start = ((), (), s32[]{:S(2)}) async-start(), calls=%async_computation.21 | async-start | bytes 17301504 | tf_op jit(solution)/shard_map/reduce_scatter | solution.py:224
  1064.2 1.2 copy-start.18
  1064.2 479.3 %reduce-scatter.15.cloned.1.call-start = ((), (), s32[]{:S(2)}) async-start(), calls=%async_computation.20 | async-start | bytes 8650752 | tf_op jit(solution)/shard_map/reduce_scatter | solution.py:223
  1070.1 1.6 copy-start.4
  1070.1 660.3 %reduce-scatter.11.cloned.1.call-start = ((), (), s32[]{:S(2)}) async-start(), calls=%async_computation.18 | async-start | bytes 17301504 | tf_op jit(solution)/shard_map/reduce_scatter | solution.py:221
  1080.6 1.0 copy-start.10
  1080.6 1089.9 %reduce-scatter.19.cloned.1.call-start = ((), (), s32[]{:S(2)}) async-start(), calls=%async_computation.22 | async-start | bytes 51904512 | tf_op jit(solution)/shard_map/reduce_scatter | solution.py:179
  1102.8 1505.1 %reduce-scatter.21.cloned.1.call-start = ((), (), s32[]{:S(2)}) async-start(), calls=%async_computation.23 | async-start | bytes 51904512 | tf_op jit(solution)/shard_map/reduce_scatter | solution.py:180
  1124.0 1.0 copy-start.21
  1124.0 1921.4 %reduce-scatter.23.cloned.1.call-start = ((), (), s32[]{:S(2)}) async-start(), calls=%async_computation.24 | async-start | bytes 51904512 | tf_op jit(solution)/shard_map/reduce_scatter | solution.py:171
  1146.2 6.6 copy-start.2
  1146.2 6.6 copy-start.13
  1152.8 11.3 copy-start.8
  1164.0 2.2 copy-start.5
  1164.0 2.5 copy-start.19
  1166.6 1.7 copy-start.22
  1166.6 43.0 %copy-start.24 = (f32[128]{0:T(128)S(1)}, f32[128]{0:T(128)}, u32[]{:S(2)}) copy-start(f32[128]{0:T(128)} %copy-done.23) | copy-start | bytes 1540
Sparse Core Ops, SparseCore 0:
  11.0 64.7 all-gather.13
  78.8 60.6 all-gather.9
  141.7 29.3 all-gather.15
  173.1 28.1 all-gather.11
  204.1 76.9 all-gather.17
  283.9 75.9 all-gather.19
  363.0 153.3 all-gather.21
  519.3 152.8 all-gather.23
  675.2 152.8 all-gather.25
  963.4 85.1 reduce-scatter.8
  1054.9 148.8 reduce-scatter.12
  1206.5 184.1 reduce-scatter.16
  1393.6 149.8 reduce-scatter.14
  1546.2 184.1 reduce-scatter.10
  1737.2 433.2 reduce-scatter.18
  2177.3 430.4 reduce-scatter.20
  2614.7 430.6 reduce-scatter.22
where the time goes:
time: 3060 us; the launch traced here: 3050 us
  waiting for transfers between devices  2580 us (84%)
  matrix products  287 us (9%)
  blocking collectives  82.6 us (3%)
  local copies, waits for them, and re-layouts  56.8 us (2%)
    reduce_scatter x1, waiting for transfers between devices, shards(): lax.psum_scatter(gate_term, ('dp', 'ctx'), scatter_dimension=0, tiled=True)  440 us
    reduce_scatter x1, waiting for transfers between devices, shards(): lax.psum_scatter(down_term, ('dp', 'ctx'), scatter_dimension=0, tiled=True)  438 us
    reduce_scatter x1, waiting for transfers between devices, shards(): lax.psum_scatter(up_term, ('dp', 'ctx'), scatter_dimension=0, tiled=True)  437 us
    reduce_scatter x1, waiting for transfers between devices, shards(): lax.psum_scatter(query_term, ('dp', 'ctx'), scatter_dimension=0, tiled=True)  187 us
    reduce_scatter x1, waiting for transfers between devices, shards(): lax.psum_scatter(out_term, ('dp', 'ctx'), scatter_dimension=0, tiled=True)  180 us
    reduce_scatter x1, waiting for transfers between devices, shards(): lax.psum_scatter(valuew_term, ('dp', 'ctx'), scatter_dimension=0, tiled=T...  153 us
    all_gather x1, waiting for transfers between devices, shards(): lax.all_gather(w_gate, ('dp', 'ctx'), axis=0, tiled=True)  151 us
    all_gather x1, waiting for transfers between devices, shards(): lax.all_gather(w_up, ('dp', 'ctx'), axis=0, tiled=True)  143 us
  transfers between devices with their start and end apart: 17, of which 16 were waited for; matrix products, arithmetic and copies ran while one was open for 7% of the time, Pallas kernels for 0%

commit v1 on v0

v1 whole, which is shorter than its diff:
```python
import jax
import jax.numpy as jnp
from jax import lax
from jax.sharding import PartitionSpec as P

QUERY_HEADS = 16
KEY_VALUE_HEADS = 8
HEAD_SIZE = 128
EPSILON = 1e-06
ROPE_BASE = 1000000.0
BF = jnp.bfloat16
F32 = jnp.float32


def rms_scale(value, gain):
    return value * lax.rsqrt(jnp.mean(value * value, -1, keepdims=True) + EPSILON) * gain


def rotate(value, cosine, sine):
    half = value.shape[-1] // 2
    first = value[..., :half]
    second = value[..., half:]
    return jnp.concatenate([first * cosine - second * sine, second * cosine + first * sine], -1)


def mm(left, right):
    return jnp.dot(left, right, preferred_element_type=F32)


def mm_tn(left, right):
    return lax.dot_general(left, right, (((0,), (0,)), ((), ())), preferred_element_type=F32)


def mm_nt(left, right):
    return lax.dot_general(left, right, (((1,), (1,)), ((), ())), preferred_element_type=F32)


def gated_unit(gate, up):
    return jax.nn.silu(gate) * up


def swap_ctx(pieces):
    return lax.all_to_all(pieces, "ctx", 0, 0)


def general(layer_input, prefix, wq, wk, wv, wo, w_gate, w_up, w_down, gains, cotangent):
    nd, nc = lax.axis_size("dp"), lax.axis_size("ctx")
    me = lax.axis_index("ctx")
    rows = layer_input.shape[1]
    seq = rows * nc
    depth, width = wq.shape[0], layer_input.shape[2]
    heads = QUERY_HEADS // nc
    copies = max(1, nc // KEY_VALUE_HEADS)
    kv_heads = max(1, KEY_VALUE_HEADS // nc)
    unit = w_down.shape[0]
    scale = HEAD_SIZE ** (-0.5)

    def columns_to(weight, parts):
        return jnp.moveaxis(weight.reshape(depth, parts, -1), 1, 0)

    def by_head(weight, repeat):
        parts = columns_to(weight, nc // repeat)
        return jnp.repeat(parts, repeat, 0) if repeat > 1 else parts

    def by_unit(weight):
        return jnp.transpose(weight.reshape(depth, nd, nc, unit), (2, 0, 1, 3)).reshape(
            nc, depth, nd * unit
        )

    def everywhere(array):
        return lax.all_gather(array, "dp", axis=0, tiled=True)

    qkv_piece = jnp.concatenate([by_head(wq, 1), by_head(wk, copies), by_head(wv, copies)], 2)
    w_qkv = everywhere(swap_ctx(qkv_piece).reshape(nc * depth, -1))
    plane = nc * wo.shape[0]
    span = QUERY_HEADS * HEAD_SIZE // nc
    need = span // wo.shape[0]
    by_plane = everywhere(wo).reshape(nd, wo.shape[0], width)
    wanted = jnp.stack([by_plane[i * span // plane] for i in range(nc)])
    arrived = swap_ctx(wanted)
    first_source = (me * span % plane) // wo.shape[0]
    w_o = lax.dynamic_slice_in_dim(arrived, first_source, need, 0).reshape(span, width)
    w_gu = everywhere(
        swap_ctx(jnp.concatenate([by_unit(w_gate), by_unit(w_up)], 2)).reshape(nc * depth, -1)
    )
    w_d = everywhere(w_down)
    gain_all = lax.all_gather(gains, ("dp", "ctx"), axis=0, tiled=True).astype(F32)
    gain_one = gain_all[:width]
    gain_two = gain_all[width : 2 * width]
    gain_q = gain_all[2 * width : 2 * width + HEAD_SIZE]
    gain_k = gain_all[2 * width + HEAD_SIZE :]

    def whole(array):
        return lax.all_gather(array, "ctx", axis=0, tiled=True)

    def own_sum(partial):
        return lax.psum_scatter(partial.astype(BF), "ctx", scatter_dimension=0, tiled=True).astype(
            F32
        )

    pos = jnp.arange(seq, dtype=jnp.int32)
    visible = (pos[None, :] <= pos[:, None]) | (pos[None, :] < prefix[0])
    freqs = ROPE_BASE ** (-(jnp.arange(HEAD_SIZE // 2, dtype=F32) * 2.0 / HEAD_SIZE))
    angles = pos.astype(F32)[:, None] * freqs[None, :]
    cosine = jnp.cos(angles)[:, None, :]
    sine = jnp.sin(angles)[:, None, :]

    def prepare_heads(raw, gain):
        return rotate(rms_scale(raw, gain), cosine, sine)

    inputs = layer_input[0].astype(F32)
    n1, back_one = jax.vjp(rms_scale, inputs, gain_one)
    n1_all = whole(n1.astype(BF))
    dy_all = whole(cotangent[0])
    qkv = mm(n1_all, w_qkv)
    q_raw = qkv[:, : heads * HEAD_SIZE].reshape(seq, heads, HEAD_SIZE)
    k_raw = qkv[:, heads * HEAD_SIZE : (heads + kv_heads) * HEAD_SIZE].reshape(
        seq, kv_heads, HEAD_SIZE
    )
    v = qkv[:, (heads + kv_heads) * HEAD_SIZE :].astype(BF).reshape(seq, kv_heads, HEAD_SIZE)
    q_rot, back_q = jax.vjp(prepare_heads, q_raw, gain_q)
    k_rot, back_k = jax.vjp(prepare_heads, k_raw, gain_k)
    q_rot = q_rot.astype(BF).reshape(seq, kv_heads, -1, HEAD_SIZE)
    k_rot = k_rot.astype(BF)
    scores = jnp.einsum("tkgd,skd->kgts", q_rot, k_rot, preferred_element_type=F32) * scale
    scores = jnp.where(visible[None, None], scores, -1e30)
    top = jnp.max(scores, -1, keepdims=True)
    expo = jnp.exp(scores - top)
    total = jnp.sum(expo, -1, keepdims=True)
    probs = expo / total
    probs_bf = probs.astype(BF)
    o = jnp.einsum("kgts,skd->tkgd", probs_bf, v, preferred_element_type=F32).astype(BF)
    o = o.reshape(seq, heads * HEAD_SIZE)
    hidden = inputs + own_sum(mm(o, w_o))
    n2, back_two = jax.vjp(rms_scale, hidden, gain_two)
    n2_all = whole(n2.astype(BF))
    gu = mm(n2_all, w_gu)
    gate, up = gu[:, : nd * unit], gu[:, nd * unit :]
    active, back_gated = jax.vjp(gated_unit, gate, up)
    active = active.astype(BF)
    output = (hidden + own_sum(mm(active, w_d))).astype(BF)
    def row_sum(term):
        return lax.psum_scatter(term.astype(BF), "dp", scatter_dimension=0, tiled=True)

    down_grad = row_sum(mm_tn(active, dy_all)).astype(F32)
    d_gate, d_up = back_gated(mm_nt(dy_all, w_d))
    d_gu = jnp.concatenate([d_gate.astype(BF), d_up.astype(BF)], 1)
    gu_sum = swap_ctx(row_sum(mm_tn(n2_all, d_gu)).reshape(nc, depth, -1)).astype(F32)
    gu_sum = gu_sum.reshape(nc, depth, 2, nd, unit)
    gu_sum = jnp.transpose(gu_sum, (2, 1, 3, 0, 4)).reshape(2, depth, -1)
    gate_grad, up_grad = gu_sum[0], gu_sum[1]
    upstream = cotangent[0].astype(F32)
    d_hidden_part, d_gain_two = back_two(own_sum(mm_nt(d_gu, w_gu)))
    d_hidden = upstream + d_hidden_part
    d_attn = whole(d_hidden.astype(BF))
    wo_term = mm_tn(o, d_attn).astype(BF).reshape(need, wo.shape[0], width)
    slots = jnp.zeros((nc, wo.shape[0], width), BF)
    slots = lax.dynamic_update_slice_in_dim(slots, wo_term, first_source, 0)
    back_home = swap_ctx(slots)
    mine = []
    for plane_index in range(nd):
        total_plane = 0
        for i in range(nc):
            if i * span // plane == plane_index:
                total_plane = total_plane + back_home[i].astype(F32)
        mine.append(total_plane)
    wo_grad = lax.psum_scatter(
        jnp.stack(mine).astype(BF), "dp", scatter_dimension=0, tiled=True
    )[0].astype(F32)
    d_o = mm_nt(d_attn, w_o).astype(BF).reshape(seq, kv_heads, -1, HEAD_SIZE)
    d_probs = jnp.einsum("tkgd,skd->kgts", d_o, v, preferred_element_type=F32)
    d_v = jnp.einsum("kgts,tkgd->skd", probs_bf, d_o, preferred_element_type=F32).astype(BF)
    d_scores = (probs * (d_probs - jnp.sum(d_probs * probs, -1, keepdims=True))).astype(BF)
    d_q = jnp.einsum("kgts,skd->tkgd", d_scores, k_rot, preferred_element_type=F32) * scale
    d_k = jnp.einsum("kgts,tkgd->skd", d_scores, q_rot, preferred_element_type=F32) * scale
    d_q, d_gain_q = back_q(d_q.reshape(seq, heads, HEAD_SIZE))
    d_k, d_gain_k = back_k(d_k)
    d_qkv = jnp.concatenate(
        [a.reshape(seq, -1).astype(BF) for a in (d_q, d_k, d_v)], 1
    )
    qkv_sum = swap_ctx(row_sum(mm_tn(n1_all, d_qkv)).reshape(nc, depth, -1)).astype(F32)
    at_k, at_v = heads * HEAD_SIZE, (heads + kv_heads) * HEAD_SIZE

    def columns_back(part, repeat):
        part = part.reshape(nc // repeat, repeat, depth, -1).sum(1)
        return jnp.moveaxis(part, 0, 1).reshape(depth, -1)

    wq_grad = columns_back(qkv_sum[:, :, :at_k], 1)
    wk_grad = columns_back(qkv_sum[:, :, at_k:at_v], copies)
    wv_grad = columns_back(qkv_sum[:, :, at_v:], copies)
    d_input_part, d_gain_one = back_one(own_sum(mm_nt(d_qkv, w_qkv)))
    x_grad = (d_hidden + d_input_part).astype(BF)
    gain_term = jnp.concatenate([d_gain_one, d_gain_two, d_gain_q, d_gain_k])
    gains_grad = lax.psum_scatter(gain_term, ("dp", "ctx"), scatter_dimension=0, tiled=True)
    return (
        output[None], x_grad[None], wq_grad, wk_grad, wv_grad, wo_grad,
        gate_grad, up_grad, down_grad, gains_grad,
    )


def solution(mesh):
    tokens = P("dp", "ctx", None)
    matrix = P(("dp", "ctx"), None)
    vector = P(("dp", "ctx"))
    return jax.shard_map(
        general,
        mesh=mesh,
        in_specs=(tokens, P("dp")) + (matrix,) * 7 + (vector, tokens),
        out_specs=(tokens, tokens) + (matrix,) * 7 + (vector,),
        check_vma=False,
    )
```

time: 3060 us -> 919 us (0.30)
  waiting for transfers between devices: 2580 us -> 415 us
  matrix products: 287 us -> 110 us
  blocking collectives: 82.6 us -> 255 us
    reduce_scatter x8 -> x7, waiting for transfers between devices: 1920 us -> 102 us  [the longest x4 102 us: own_sum(): lax.psum_scatter(partial.astype(BF), 'ctx', scatter_dimension=0, tiled=True)]
    all_gather x9 -> x8, waiting for transfers between devices: 660 us -> 235 us  [the longest x4 135 us: whole(): return lax.all_gather(array, 'ctx', axis=0, tiled=True)]
    dot_general x77 -> x18, matrix products: 287 us -> 110 us  [the longest x4 31.3 us: mm_nt(): lax.dot_general(left, right, (((1,), (1,)), ((), ())), preferred_element_...]
    all_to_all x0 -> x4, blocking collectives: none -> 174 us  [swap_ctx(): return lax.all_to_all(pieces, 'ctx', 0, 0)]
    all_to_all x0 -> x2, waiting for transfers between devices: none -> 73.7 us  [swap_ctx(): return lax.all_to_all(pieces, 'ctx', 0, 0)]
  transfers between devices with their start and end apart: 17 -> 18, of which waited for: 16 -> 10; matrix products, arithmetic and copies ran while one was open for 7% -> 17% of each run, Pallas kernels for 0% -> 0%
where the time goes in v1:
time: 919 us; the launch traced here: 912 us
  waiting for transfers between devices  415 us (45%)
  blocking collectives  255 us (28%)
  matrix products  110 us (12%)
  local copies, waits for them, and re-layouts  68.4 us (7%)
  other arithmetic  36.6 us (4%)
  between operations  15.8 us (2%)
  starting transfers between devices  11.3 us (1%)
    all_to_all x4, blocking collectives, swap_ctx(): return lax.all_to_all(pieces, 'ctx', 0, 0)  174 us
    all_gather x4, waiting for transfers between devices, whole(): return lax.all_gather(array, 'ctx', axis=0, tiled=True)  135 us
    reduce_scatter x4, waiting for transfers between devices, own_sum(): lax.psum_scatter(partial.astype(BF), 'ctx', scatter_dimension=0, tiled=True)  102 us
    all_gather x4, waiting for transfers between devices, everywhere(): return lax.all_gather(array, 'dp', axis=0, tiled=True)  99.4 us
    unnamed x2, blocking collectives  81 us
    all_to_all x2, waiting for transfers between devices, swap_ctx(): return lax.all_to_all(pieces, 'ctx', 0, 0)  73.7 us
    dot_general x4, matrix products, mm_nt(): lax.dot_general(left, right, (((1,), (1,)), ((), ())), preferred_element_...  31.3 us
    dot_general x4, matrix products, mm(): return jnp.dot(left, right, preferred_element_type=F32)  28.1 us
  transfers between devices with their start and end apart: 18, of which 10 were waited for; matrix products, arithmetic and copies ran while one was open for 17% of the time, Pallas kernels for 0%

profile of v1, /device:TPU:1, one launch (start us, length us, event | category | flops | bytes accessed | tf_op | source)
XLA Modules:
  0.0 911.8 jit_solution(3456855965065906383)
XLA Ops:
  11.1 20.6 %all_to_all.30 = bf16[8,64,512]{2,1,0:T(8,128)(2,1)} all-to-all(bf16[8,64,512]{2,1,0:T(8,128)(2,1)S(1)} %copy.84), channel_id=1, replica_groups=mesh['dp'=4,'ctx'=8] {'ctx'}, dimensions={0} | all-to-all | bytes 1048576 | tf_op jit(solution)/shard_map/all_to_all | solution.py:43
  32.0 39.1 %all-reduce.4 = bf16[4352]{0:T(1024)(128)(2,1)S(1)} all-reduce(bf16[4352]{0:T(1024)(128)(2,1)S(1)} %dynamic-update-slice), channel_id=1, replica_groups=mesh['dp'=4,'ctx'=8] {'dp','ctx'}, use_global_device_ids=true, to_apply=%add.4 | all-reduce | flops 4352 | bytes 17408
  73.5 1.7 fusion.74
  75.2 1.7 fusion.75
  78.5 1.7 fusion.77
  80.2 1.7 fusion.78
  81.9 1.7 fusion.79
  83.6 1.7 fusion.80
  85.2 1.7 fusion.81
  86.9 4.9 all-to-all-start.1
  92.8 3.0 multiply_cosine_fusion
  96.1 73.7 %all-to-all-done.1 = bf16[8,64,2048]{2,1,0:T(8,128)(2,1)} async-done(((bf16[8,64,2048]{2,1,0:T(8,128)(2,1)}), bf16[8,64,2048]{2,1,0:T(8,128)(2,1)}, u32[]{:S(2)}, u32[]{:S(2)}) %all-to-all-start.1) | async-done | bytes 2097184 | tf_op jit(solution)/shard_map/all_to_all | solution.py:43
  169.8 2.4 constant_dynamic-slice_fusion
  172.2 5.2 fusion.105
  183.7 2.2 fusion.5
  185.9 2.0 fusion.4
  189.1 4.1 fusion.25
  193.3 3.3 convolution_convert_fusion.3
  196.9 3.0 reshape.439
  199.9 2.6 copy.131
  202.5 3.0 reshape.440
  205.5 3.0 reshape.441
  208.5 2.6 copy.130
  211.1 3.0 reshape.442
  215.6 60.3 %all_to_all.31 = bf16[8,64,1536]{2,1,0:T(8,128)(2,1)} all-to-all(bf16[8,64,1536]{2,1,0:T(8,128)(2,1)S(1)} %pad_maximum_fusion.3), channel_id=1, replica_groups=mesh['dp'=4,'ctx'=8] {'ctx'}, dimensions={0} | all-to-all | bytes 3145728 | tf_op jit(solution)/shard_map/all_to_all | solution.py:43
  277.3 2.0 multiply_convert_fusion.2
  281.4 66.9 %all-gather.18.cloned.1.call-done = bf16[2048,1536]{1,0:T(8,128)(2,1)} async-done(((bf16[512,1536]{1,0:T(8,128)(2,1)}), bf16[2048,1536]{1,0:T(8,128)(2,1)}) %all-gather.18.cloned.1.call-update) | async-done | bytes 6291472 | tf_op jit(solution)/shard_map/all_gather | solution.py:71
  348.3 49.6 %all-gather.16.cloned.1.call-done = bf16[1024,2048]{1,0:T(8,128)(2,1)} async-done(((bf16[128,2048]{1,0:T(8,128)(2,1)}), bf16[1024,2048]{1,0:T(8,128)(2,1)}) %all-gather.16.cloned.1.call-update) | async-done | bytes 4194320 | tf_op jit(solution)/shard_map/all_gather | solution.py:94
  397.9 11.7 %fusion.106 = f32[1024,1536]{1,0:T(8,128)} fusion(bf16[1024,2048]{1,0:T(8,128)(2,1)} %all-gather.16.cloned.1.call-done, bf16[2048,1536]{1,0:T(8,128)(2,1)} %all-gather.18.cloned.1.call-done), kind=kOutput, calls=%fused_computation.184 | convolution fusion | flops 6442450944 | bytes 16777216 | tf_op jit(solution)/shard_map/dot_general | solution.py:27
  409.7 32.4 %all-gather.20.cloned.1.call-done = bf16[768,2048]{1,0:T(8,128)(2,1)} async-done(((bf16[192,2048]{1,0:T(8,128)(2,1)}), bf16[768,2048]{1,0:T(8,128)(2,1)}) %all-gather.20.cloned.1.call-update) | async-done | bytes 3145744 | tf_op jit(solution)/shard_map/all_gather | solution.py:71
  442.1 49.2 %all-gather.24.cloned.1.call-done = bf16[1,1024,2048]{2,1,0:T(8,128)(2,1)} async-done(((bf16[1,128,2048]{2,1,0:T(8,128)(2,1)}), bf16[1,1024,2048]{2,1,0:T(8,128)(2,1)}) %all-gather.24.cloned.1.call-update) | async-done | bytes 4194320 | tf_op jit(solution)/shard_map/all_gather | solution.py:94
  491.3 10.5 %fusion.21 = (bf16[1024,768]{1,0:T(8,128)(2,1)S(1)}, bf16[1024,768]{1,0:T(8,128)(2,1)S(1)}, bf16[1024,768]{1,0:T(8,128)(2,1)}) fusion(f32[1024,1536]{1,0:T(8,128)} %fusion.106, bf16[768,2048]{1,0:T(8,128)(2,1)} %all-gather.20.cloned.1.call-done, bf16[1,1024,2048]{2,1,0:T(8,128)(2,1)} %all-gather.24.cloned.1.call-done), kind=kOutput, calls=%fused_computation.31 | convolution fusion | flops 3233808384 | bytes 18350080 | tf_op jit(solution)/shard_map/dot_general | solution.py:35
  503.4 11.0 %convolution_convert_fusion.1 = bf16[1024,2048]{1,0:T(8,128)(2,1)} fusion(bf16[2048,1536]{1,0:T(8,128)(2,1)} %all-gather.18.cloned.1.call-done, bf16[1024,768]{1,0:T(8,128)(2,1)S(1)} %get-tuple-element.19, bf16[1024,768]{1,0:T(8,128)(2,1)S(1)} %get-tuple-element.18), kind=kOutput, calls=%fused_computation.24 | convolution fusion | flops 6450839552 | bytes 13631488 | tf_op jit(solution)/shard_map/dot_general | solution.py:35
  514.5 46.3 %reduce-scatter.15.cloned.1.call-done = bf16[128,2048]{1,0:T(8,128)(2,1)} async-done(((bf16[1024,2048]{1,0:T(8,128)(2,1)}), bf16[128,2048]{1,0:T(8,128)(2,1)}) %reduce-scatter.15.cloned.1.call-update) | async-done | bytes 524304 | tf_op jit(solution)/shard_map/reduce_scatter | solution.py:97
  562.3 2.4 fusion.99
  564.9 11.2 %convolution_convert_fusion = bf16[2048,1536]{1,0:T(8,128)(2,1)} fusion(bf16[1024,2048]{1,0:T(8,128)(2,1)} %all-gather.16.cloned.1.call-done, bf16[1024,768]{1,0:T(8,128)(2,1)} %copy-done.29, bf16[1024,768]{1,0:T(8,128)(2,1)} %copy-done.28), kind=kOutput, calls=%fused_computation.7 | convolution fusion | flops 6451888128 | bytes 13631488 | tf_op jit(solution)/shard_map/dot_general | solution.py:31
  576.3 36.5 %all-gather.22.cloned.1.call-done = bf16[1024,2048]{1,0:T(8,128)(2,1)} async-done(((bf16[128,2048]{1,0:T(8,128)(2,1)}), bf16[1024,2048]{1,0:T(8,128)(2,1)}) %all-gather.22.cloned.1.call-update) | async-done | bytes 4194320 | tf_op jit(solution)/shard_map/all_gather | solution.py:94
  612.8 3.8 convolution_convert_fusion.7
  616.6 5.7 fusion
  623.9 2.8 fusion.6
  626.7 1.8 fusion.24
  630.1 1.7 fusion.48
  633.1 4.5 fusion.36
  639.2 5.7 fusion.40
  645.6 3.8 convolution_convert_fusion.5
  649.5 7.8 fusion.16
  657.5 3.5 convolution_convert_fusion.6
  661.4 51.0 %all_to_all.32 = bf16[8,64,2048]{2,1,0:T(8,128)(2,1)S(1)} all-to-all(bf16[8,64,2048]{2,1,0:T(8,128)(2,1)S(1)} %constant_dynamic-update-slice_fusion), channel_id=1, replica_groups=mesh['dp'=4,'ctx'=8] {'ctx'}, dimensions={0} | all-to-all | bytes 4194304 | tf_op jit(solution)/shard_map/all_to_all | solution.py:43
  714.0 6.0 convolution_convert_fusion.2
  720.3 7.8 convolution_convert_fusion.4
  728.1 42.1 %all_to_all.33 = bf16[8,64,1536]{2,1,0:T(8,128)(2,1)} all-to-all(bf16[8,64,1536]{2,1,0:T(8,128)(2,1)} %bitcast.265), channel_id=1, replica_groups=mesh['dp'=4,'ctx'=8] {'ctx'}, dimensions={0} | all-to-all | bytes 3145728 | tf_op jit(solution)/shard_map/all_to_all | solution.py:43
  770.3 4.4 all-to-all-start.3
  774.7 2.5 convert_element_type.253
  777.2 5.8 reshape.458
  782.9 4.8 copy.129
  787.7 2.3 fusion.102
  790.1 3.0 squeeze.11
  793.0 3.0 squeeze.10
  797.9 2.5 reduce-scatter.25.cloned.1.call-done
  800.4 1.8 bitcast_convert_fusion
  802.2 48.3 %reduce-scatter.17.cloned.1.call-done = bf16[128,2048]{1,0:T(8,128)(2,1)} async-done(((bf16[1024,2048]{1,0:T(8,128)(2,1)}), bf16[128,2048]{1,0:T(8,128)(2,1)}) %reduce-scatter.17.cloned.1.call-update) | async-done | bytes 524304 | tf_op jit(solution)/shard_map/reduce_scatter | solution.py:97
  852.0 41.9 %all-reduce.6 = f32[4352]{0:T(1024)S(1)} all-reduce(f32[4352]{0:T(1024)S(1)} %pad_maximum_fusion.12), channel_id=11, replica_groups=mesh['dp'=4,'ctx'=8] {'dp','ctx'}, use_global_device_ids=true, to_apply=%region_23.24.clone | all-reduce | flops 4352 | bytes 34816
  894.6 7.2 reduce-scatter.13.cloned.1.call-done
  901.8 3.0 fusion.55
  (158 shorter events, 38.1 us)
Async XLA Ops:
  7.2 24.6 %copy-start.23 = (bf16[136]{0:T(256)(128)(2,1)S(1)}, bf16[136]{0:T(256)(128)(2,1)}, u32[]{:S(2)}) copy-start(bf16[136]{0:T(256)(128)(2,1)} %param.20) | copy-start | bytes 820
  7.2 63.9 %copy-start.2 = (bf16[1,128,2048]{2,1,0:T(8,128)(2,1)S(1)}, bf16[1,128,2048]{2,1,0:T(8,128)(2,1)}, u32[]{:S(2)}) copy-start(bf16[1,128,2048]{2,1,0:T(8,128)(2,1)} %param.11) | copy-start | bytes 1572868
  7.2 66.3 %all-gather.14.cloned.1.call-start = ((), (), s32[]{:S(2)}) async-start(), calls=%async_computation.16 | async-start | bytes 1310720 | tf_op jit(solution)/shard_map/all_gather | solution.py:71
  7.9 164.2 %all-gather.12.cloned.1.call-start = ((), (), s32[]{:S(2)}) async-start(), calls=%async_computation.15 | async-start | bytes 2621440 | tf_op jit(solution)/shard_map/all_gather | solution.py:71
  31.7 140.5 %all-gather.10.cloned.1.call-start = ((), (), s32[]{:S(2)}) async-start(), calls=%async_computation.14 | async-start | bytes 4718592 | tf_op jit(solution)/shard_map/all_gather | solution.py:94
  71.3 0.6 copy-start.20
  71.9 15.1 %copy-start.18 = (f32[128]{0:T(128)}, f32[128]{0:T(128)S(1)}, u32[]{:S(2)}) copy-start(f32[128]{0:T(128)S(1)} %fusion.90) | copy-start | bytes 1540
  71.9 0.6 copy-start.16
  86.9 82.9 %all-to-all-start.1 = ((bf16[8,64,2048]{2,1,0:T(8,128)(2,1)}), bf16[8,64,2048]{2,1,0:T(8,128)(2,1)}, u32[]{:S(2)}, u32[]{:S(2)}) async-start(bf16[8,64,2048]{2,1,0:T(8,128)(2,1)} %fusion.81), calls=%async_computation.1 | async-start | bytes 4194304 | tf_op jit(solution)/shard_map/all_to_all | solution.py:43
  91.8 184.2 %reduce-scatter.11.cloned.1.call-start = ((), (), s32[]{:S(2)}) async-start(), calls=%async_computation.17 | async-start | bytes 4718592 | tf_op jit(solution)/shard_map/reduce_scatter | solution.py:97
  95.7 86.4 %copy-start.8 = (f32[1024,64]{1,0:T(8,128)}, f32[1024,64]{1,0:T(8,128)S(1)}, u32[]{:S(2)}) copy-start(f32[1024,64]{1,0:T(8,128)S(1)} %get-tuple-element.43) | copy-start | bytes 786436
  177.4 2.8 copy-start.4
  183.6 2.2 copy-start.12
  183.6 2.2 copy-start.13
  185.9 3.3 copy-start.1
  189.1 4.2 copy-start.11
  193.3 3.3 copy-start.14
  196.6 151.7 %all-gather.18.cloned.1.call-start = ((), (), s32[]{:S(2)}) async-start(), calls=%async_computation.19 | async-start | bytes 7864320 | tf_op jit(solution)/shard_map/all_gather | solution.py:71
  275.9 122.0 %all-gather.16.cloned.1.call-start = ((), (), s32[]{:S(2)}) async-start(), calls=%async_computation.18 | async-start | bytes 4718592 | tf_op jit(solution)/shard_map/all_gather | solution.py:94
  279.4 162.7 %all-gather.20.cloned.1.call-start = ((), (), s32[]{:S(2)}) async-start(), calls=%async_computation.20 | async-start | bytes 3932160 | tf_op jit(solution)/shard_map/all_gather | solution.py:71
  280.1 211.1 %all-gather.24.cloned.1.call-start = ((), (), s32[]{:S(2)}) async-start(), calls=%async_computation.28 | async-start | bytes 4718592 | tf_op jit(solution)/shard_map/all_gather | solution.py:94
  280.9 279.9 %reduce-scatter.15.cloned.1.call-start = ((), (), s32[]{:S(2)}) async-start(), calls=%async_computation.22 | async-start | bytes 4718592 | tf_op jit(solution)/shard_map/reduce_scatter | solution.py:97
  501.7 1.1 copy-start.28
  501.7 1.7 copy-start.29
  514.4 46.4 %copy-start.3 = (bf16[128,2048]{1,0:T(8,128)(2,1)S(1)}, bf16[128,2048]{1,0:T(8,128)(2,1)}, u32[]{:S(2)}) copy-start(bf16[128,2048]{1,0:T(8,128)(2,1)} %reduce-scatter.11.cloned.1.call-done) | copy-start | bytes 1572868
  514.5 98.3 %all-gather.22.cloned.1.call-start = ((), (), s32[]{:S(2)}) async-start(), calls=%async_computation.23 | async-start | bytes 4718592 | tf_op jit(solution)/shard_map/all_gather | solution.py:94
  564.8 163.3 %reduce-scatter.21.cloned.1.call-start = ((), (), s32[]{:S(2)}) async-start(), calls=%async_computation.26 | async-start | bytes 7864320 | tf_op jit(solution)/shard_map/reduce_scatter | solution.py:143
  576.1 194.2 %reduce-scatter.19.cloned.1.call-start = ((), (), s32[]{:S(2)}) async-start(), calls=%async_computation.25 | async-start | bytes 2621440 | tf_op jit(solution)/shard_map/reduce_scatter | solution.py:143
  616.6 5.7 copy-start.24
  616.6 5.7 slice-start
  616.6 7.3 slice-start.1
  626.7 2.5 copy-start
  626.7 1.9 copy-start.9
  626.7 2.0 copy-start.10
  633.1 5.7 copy-start.5
  633.1 6.1 copy-start.25
  639.2 6.5 copy-start.22
  644.9 0.7 copy-start.26
  649.5 125.3 %reduce-scatter.23.cloned.1.call-start = ((), (), s32[]{:S(2)}) async-start(), calls=%async_computation.27 | async-start | bytes 3932160 | tf_op jit(solution)/shard_map/reduce_scatter | solution.py:143
  649.5 7.9 copy-start.15
  657.4 143.0 %reduce-scatter.25.cloned.1.call-start = ((), (), s32[]{:S(2)}) async-start(), calls=%async_computation.29 | async-start | bytes 1310720
  712.3 1.6 copy-start.27
  713.9 136.5 %reduce-scatter.17.cloned.1.call-start = ((), (), s32[]{:S(2)}) async-start(), calls=%async_computation.24 | async-start | bytes 4718592 | tf_op jit(solution)/shard_map/reduce_scatter | solution.py:97
  720.0 181.8 %reduce-scatter.13.cloned.1.call-start = ((), (), s32[]{:S(2)}) async-start(), calls=%async_computation.21 | async-start | bytes 4718592 | tf_op jit(solution)/shard_map/reduce_scatter | solution.py:97
  770.3 25.7 %all-to-all-start.3 = ((bf16[8,64,512]{2,1,0:T(8,128)(2,1)}), bf16[8,64,512]{2,1,0:T(8,128)(2,1)S(1)}, u32[]{:S(2)}, u32[]{:S(2)}) async-start(bf16[8,64,512]{2,1,0:T(8,128)(2,1)} %bitcast.270), calls=%async_computation.8 | async-start | bytes 1048576 | tf_op jit(solution)/shard_map/all_to_all | solution.py:43
  796.0 54.4 %copy-start.17 = (f32[2048]{0:T(1024)S(1)}, f32[2048]{0:T(1024)}, u32[]{:S(2)}) copy-start(f32[2048]{0:T(1024)} %copy-done.16) | copy-start | bytes 24580
  796.0 54.4 %copy-start.19 = (f32[128]{0:T(128)S(1)}, f32[128]{0:T(128)}, u32[]{:S(2)}) copy-start(f32[128]{0:T(128)} %copy-done.18) | copy-start | bytes 1540
  796.0 98.6 %copy-start.21 = (f32[128]{0:T(128)S(1)}, f32[128]{0:T(128)}, u32[]{:S(2)}) copy-start(f32[128]{0:T(128)} %copy-done.20) | copy-start | bytes 1540
  796.0 105.8 %copy-start.6 = (bf16[1,128,2048]{2,1,0:T(8,128)(2,1)S(1)}, bf16[1,128,2048]{2,1,0:T(8,128)(2,1)}, u32[]{:S(2)}) copy-start(bf16[1,128,2048]{2,1,0:T(8,128)(2,1)} %param.21) | copy-start | bytes 1572868
  796.0 105.8 %copy-start.7 = (bf16[128,2048]{1,0:T(8,128)(2,1)S(1)}, bf16[128,2048]{1,0:T(8,128)(2,1)}, u32[]{:S(2)}) copy-start(bf16[128,2048]{1,0:T(8,128)(2,1)} %reduce-scatter.15.cloned.1.call-done) | copy-start | bytes 1572868
Sparse Core Ops, SparseCore 0:
  9.9 28.9 all-gather.13
  40.7 36.2 all-gather.11
  79.2 84.6 all-gather.9
  196.7 68.6 reduce-scatter.10
  276.0 72.2 all-gather.17
  350.3 47.5 all-gather.15
  399.7 42.2 all-gather.19
  443.7 47.5 all-gather.23
  514.6 46.1 reduce-scatter.14
  564.9 47.8 all-gather.21
  615.8 68.4 reduce-scatter.20
  687.1 35.1 reduce-scatter.18
  725.6 43.9 reduce-scatter.22
  772.6 27.7 reduce-scatter.24
  802.5 47.8 reduce-scatter.16
  852.6 49.1 reduce-scatter.12

commit v2 on v1

--- a/solution.py
+++ b/solution.py
@@ -1,6 +1,9 @@
 import jax
 import jax.numpy as jnp
+import numpy as np
 from jax import lax
+from jax.experimental import pallas as pl
+from jax.experimental.pallas import tpu as pltpu
 from jax.sharding import PartitionSpec as P
 
 QUERY_HEADS = 16
@@ -198,12 +201,1658 @@
     )
 
 
+MESH = pl.DeviceIdType.MESH
+BLOCK = 128
+VMEM_BYTES = 64 << 20
+
+
+class Copies:
+    def __init__(self, sends, receives):
+        self.sends, self.receives = sends, receives
+        self.used = 0
+
+    def take(self, count=1):
+        first = self.used
+        self.used += count
+        if self.used > SLOTS:
+            raise ValueError("more semaphores")
+        return first
+
+    def to(self, src, dst, device, slot, receive_slot=None):
+        receive_slot = slot if receive_slot is None else receive_slot
+        return pltpu.make_async_remote_copy(
+            src_ref=src,
+            dst_ref=dst,
+            send_sem=self.sends.at[slot],
+            recv_sem=self.receives.at[receive_slot],
+            device_id=device,
+            device_id_type=MESH,
+        )
+
+    def here(self, src, dst, slot):
+        return pltpu.make_async_copy(src, dst, self.sends.at[slot])
+
+
+class Place:
+    def __init__(self):
+        self.d = lax.axis_index("dp")
+        self.c = lax.axis_index("ctx")
+        self.z = self.c // 2
+        self.p = lax.rem(self.c, 2)
+
+    def at(self, d, c):
+        return (d, c)
+
+
+def meet():
+    barrier = pltpu.get_barrier_semaphore()
+    d, c = lax.axis_index("dp"), lax.axis_index("ctx")
+    partners = [(d, c ^ rel) for rel in range(1, 8)]
+    partners += [(d ^ rel, c ^ twin) for rel in range(1, 4) for twin in range(2)]
+    for partner in partners:
+        pl.semaphore_signal(barrier, inc=1, device_id=partner, device_id_type=MESH)
+    pl.semaphore_wait(barrier, len(partners))
+
+
+def when(condition, then):
+    if isinstance(condition, bool):
+        if condition:
+            then()
+    else:
+        pl.when(condition)(then)
+
+
+def rows_at(start, size):
+    return pl.ds(pl.multiple_of(start, 16), size)
+
+
+class Gather:
+    def __init__(self, copies, place, buf, parts=2):
+        self.k, self.g, self.buf, self.parts = copies, place, buf, parts
+        self.size = BLOCK // parts
+        self.right = copies.take(3 * parts)
+        self.left = copies.take(3 * parts)
+        self.twin = copies.take(7 * parts)
+
+    def piece(self, z, p, part):
+        return self.buf.at[rows_at((2 * z + p) * BLOCK + part * self.size, self.size)]
+
+    def line(self, step, part, rightwards):
+        g = self.g
+        z = g.z - step if rightwards else g.z + step
+        slot = (self.right if rightwards else self.left) + step * self.parts + part
+        piece = self.piece(z, g.p, part)
+        to = g.c + 2 if rightwards else g.c - 2
+        return self.k.to(piece, piece, (g.d, to), slot)
+
+    def wait_line(self, step, part, rightwards):
+        piece = self.piece(self.g.z, self.g.p, part)
+        slot = (self.right if rightwards else self.left) + step * self.parts + part
+        self.k.to(piece, piece, (self.g.d, self.g.c ^ 1), slot).wait_recv()
+
+    def twins(self, order, z, part):
+        piece = self.piece(z, self.g.p, part)
+        return self.k.to(piece, piece, (self.g.d, self.g.c ^ 1), self.twin + order * self.parts + part)
+
+    def can_send(self, step, rightwards):
+        z = self.g.z
+        return (z >= step) & (z < 3) if rightwards else (z + step <= 3) & (z > 0)
+
+    def gets(self, step, rightwards):
+        z = self.g.z
+        return z >= step + 1 if rightwards else z + step + 1 <= 3
+
+    def start(self):
+        for part in range(self.parts):
+            self.start_part(part)
+
+    def start_part(self, part):
+        for rightwards in (True, False):
+
+            @pl.when(self.can_send(0, rightwards))
+            def _():
+                self.line(0, part, rightwards).start()
+
+        self.twins(0, self.g.z, part).start()
+
+    def start_line(self, right, left):
+        for part in range(self.parts):
+            for now, rightwards in ((right, True), (left, False)):
+
+                @pl.when(now & self.can_send(0, rightwards))
+                def _():
+                    self.line(0, part, rightwards).start()
+
+    def start_twin(self):
+        for part in range(self.parts):
+            self.twins(0, self.g.z, part).start()
+
+    def step(self, step):
+        for part in range(self.parts):
+            self.step_part(step, part)
+
+    def step_part(self, step, part):
+        for side, rightwards in enumerate((True, False)):
+            z = self.g.z - 1 - step if rightwards else self.g.z + 1 + step
+
+            @pl.when(self.gets(step, rightwards))
+            def _():
+                self.wait_line(step, part, rightwards)
+
+                def on():
+                    @pl.when(self.can_send(step + 1, rightwards))
+                    def _():
+                        self.line(step + 1, part, rightwards).start()
+
+                when(step < 2, on)
+                self.twins(1 + 2 * step + side, z, part).start()
+
+    def twin_own(self):
+        for part in range(self.parts):
+            self.twins(0, self.g.z, part).wait_recv()
+
+    def twin_step(self, step):
+        for part in range(self.parts):
+            for side, rightwards in enumerate((True, False)):
+
+                @pl.when(self.gets(step, rightwards))
+                def _():
+                    self.twins(1 + 2 * step + side, self.g.z, part).wait_recv()
+
+    def drain(self):
+        for part in range(self.parts):
+            self.twins(0, self.g.z, part).wait_send()
+            for step in range(3):
+                for side, rightwards in enumerate((True, False)):
+
+                    @pl.when(self.can_send(step, rightwards))
+                    def _():
+                        self.line(step, part, rightwards).wait_send()
+
+                    @pl.when(self.gets(step, rightwards))
+                    def _():
+                        self.twins(1 + 2 * step + side, self.g.z, part).wait_send()
+
+
+def add_rows(dst, dst_row, a, a_row, b, b_row, count):
+    def body(i, carry):
+        at = i * 32
+        total = a[rows_at(a_row + at, 32), :].astype(F32) + b[rows_at(b_row + at, 32), :].astype(F32)
+        dst[rows_at(dst_row + at, 32), :] = total.astype(dst.dtype)
+        return carry
+
+    lax.fori_loop(0, count // 32, body, 0)
+
+
+class Scatter:
+    def __init__(self, copies, place, partial, from_twin, from_left, from_right, parts=2):
+        self.k, self.g = copies, place
+        self.partial, self.from_twin = partial, from_twin
+        self.from_line = {True: from_left, False: from_right}
+        self.parts, self.size = parts, BLOCK // parts
+        self.twin = copies.take(4)
+        self.slots = {True: copies.take(3 * parts), False: copies.take(3 * parts)}
+
+    def row(self, z, p):
+        return (2 * z + p) * BLOCK
+
+    def twins(self, z, slot):
+        g = self.g
+        src = self.partial.at[rows_at(self.row(z, 1 - g.p), BLOCK)]
+        dst = self.from_twin.at[rows_at(z * BLOCK, BLOCK)]
+        return self.k.to(src, dst, (g.d, g.c ^ 1), self.twin + slot)
+
+    def send_twin(self, z):
+        self.twins(z, z).start()
+
+    def take_twin(self, z):
+        self.twins(z, z).wait_recv()
+        at = self.row(z, self.g.p)
+        add_rows(self.partial, at, self.partial, at, self.from_twin, z * BLOCK, BLOCK)
+
+    def target(self, step, rightwards):
+        return self.g.z + 3 - step if rightwards else self.g.z - 3 + step
+
+    def can_send(self, step, rightwards):
+        z = self.g.z
+        return z <= step if rightwards else 3 - z <= step
+
+    def gets(self, step, rightwards):
+        z = self.g.z
+        return (z >= 1) & (z - 1 <= step) if rightwards else (z <= 2) & (2 - z <= step)
+
+    def line(self, step, rightwards, part):
+        g = self.g
+        at = self.row(self.target(step, rightwards), g.p) + part * self.size
+        src = self.partial.at[rows_at(at, self.size)]
+        dst = self.from_line[rightwards].at[rows_at(step * BLOCK + part * self.size, self.size)]
+        slot = self.slots[rightwards] + step * self.parts + part
+        return self.k.to(src, dst, (g.d, g.c + 2 if rightwards else g.c - 2), slot)
+
+    def wait_line(self, step, rightwards, part):
+        src = self.partial.at[pl.ds(0, self.size)]
+        dst = self.from_line[rightwards].at[rows_at(step * BLOCK + part * self.size, self.size)]
+        slot = self.slots[rightwards] + step * self.parts + part
+        self.k.to(src, dst, (self.g.d, self.g.c ^ 1), slot).wait_recv()
+
+    def send(self, step, part):
+        for rightwards in (True, False):
+
+            @pl.when(self.can_send(step, rightwards))
+            def _():
+                self.line(step, rightwards, part).start()
+
+    def start(self):
+        for part in range(self.parts):
+            self.send(0, part)
+
+    def advance(self, step):
+        for part in range(self.parts):
+            for rightwards in (True, False):
+
+                @pl.when(self.gets(step, rightwards))
+                def _():
+                    self.wait_line(step, rightwards, part)
+
+                    def add():
+                        z = self.g.z + 2 - step if rightwards else self.g.z - 2 + step
+                        at = self.row(z, self.g.p) + part * self.size
+                        add_rows(
+                            self.partial, at, self.partial, at, self.from_line[rightwards],
+                            step * BLOCK + part * self.size, self.size,
+                        )
+
+                    when(step < 2, add)
+
+            when(step < 2, lambda: self.send(step + 1, part))
+
+    def finish(self, done, slot=2, part=None):
+        g = self.g
+        own = self.row(g.z, g.p)
+        first, count = (0, BLOCK) if part is None else (part * self.size, self.size)
+
+        def body(i, carry):
+            at = first + i * 16
+            total = self.partial[rows_at(own + at, 16), :].astype(F32)
+            a = self.from_line[True][rows_at(slot * BLOCK + at, 16), :].astype(F32)
+            b = self.from_line[False][rows_at(slot * BLOCK + at, 16), :].astype(F32)
+            total = total + jnp.where(g.z >= 1, a, 0.0) + jnp.where(g.z <= 2, b, 0.0)
+            done(at, total)
+            return carry
+
+        lax.fori_loop(0, count // 16, body, 0)
+
+    def send_ends(self, part, *steps):
+        for rightwards in (True, False):
+
+            @pl.when(self.g.z == (0 if rightwards else 3))
+            def _():
+                for step in steps:
+                    self.line(step, rightwards, part).start()
+
+    def relay(self, step, part):
+        for rightwards in (True, False):
+
+            @pl.when(self.gets(step, rightwards))
+            def _():
+                self.wait_line(step, rightwards, part)
+                z = self.g.z + 2 - step if rightwards else self.g.z - 2 + step
+                at = self.row(z, self.g.p) + part * self.size
+                add_rows(
+                    self.partial, at, self.partial, at, self.from_line[rightwards],
+                    step * BLOCK + part * self.size, self.size,
+                )
+                self.line(step + 1, rightwards, part).start()
+
+    def last(self, done, part):
+        for rightwards in (True, False):
+
+            @pl.when(self.gets(2, rightwards))
+            def _():
+                self.wait_line(2, rightwards, part)
+
+        self.finish(done, part=part)
+
+    def drain(self):
+        for z in range(4):
+            self.twins(z, z).wait_send()
+        for step in range(3):
+            for part in range(self.parts):
+                for rightwards in (True, False):
+
+                    @pl.when(self.can_send(step, rightwards))
+                    def _():
+                        self.line(step, rightwards, part).wait_send()
+
+
+class Outwards(Scatter):
+    def __init__(self, *args):
+        super().__init__(*args, parts=1)
+
+    def can_send(self, step, rightwards):
+        return self.g.z + 1 + step <= 3 if rightwards else self.g.z - 1 - step >= 0
+
+    def target(self, step, rightwards):
+        return self.g.z + 1 + step if rightwards else self.g.z - 1 - step
+
+    def send_ends(self, step):
+        for rightwards in (True, False):
+
+            @pl.when(self.g.z == (0 if rightwards else 3))
+            def _():
+                self.line(step, rightwards, 0).start()
+
+    def relay(self, step, chip):
+        for rightwards in (True, False):
+
+            @pl.when(self.g.z == (chip if rightwards else 3 - chip))
+            def _():
+                self.wait_line(step, rightwards, 0)
+                at = self.row(self.target(step - 1, rightwards), self.g.p)
+                add_rows(
+                    self.partial, at, self.partial, at, self.from_line[rightwards], step * BLOCK, BLOCK
+                )
+                self.line(step - 1, rightwards, 0).start()
+
+    def take_own(self):
+        for rightwards in (True, False):
+
+            @pl.when(self.g.z >= 1 if rightwards else self.g.z <= 2)
+            def _():
+                self.wait_line(0, rightwards, 0)
+
+
+class Spread:
+    def __init__(self, copies, place, piece):
+        self.k, self.g, self.piece = copies, place, piece
+        self.slots = copies.take(6)
+
+    def direct(self, half, rel):
+        g = self.g
+        piece = self.piece(g.d, half)
+        return self.k.to(piece, piece, (g.d ^ rel, g.c), self.slots + 2 * (rel - 1) + half)
+
+    def passed(self, rel):
+        g = self.g
+        piece = self.piece(g.d ^ (3 - rel), rel - 1)
+        return self.k.to(piece, piece, (g.d ^ rel, g.c), self.slots + 4 + rel - 1)
+
+    def start(self):
+        for half, rel in ((0, 1), (1, 2), (1, 1), (0, 2)):
+            self.direct(half, rel).start()
+
+    def forward(self):
+        self.direct(1, 1).wait_recv()
+        self.passed(2).start()
+        self.direct(0, 2).wait_recv()
+        self.passed(1).start()
+
+    def finish(self):
+        self.direct(0, 1).wait_recv()
+        self.direct(1, 2).wait_recv()
+        self.passed(1).wait_recv()
+        self.passed(2).wait_recv()
+
+    def drain(self):
+        for half, rel in ((0, 1), (1, 2), (1, 1), (0, 2)):
+            self.direct(half, rel).wait_send()
+        self.passed(1).wait_send()
+        self.passed(2).wait_send()
+
+
+class Direct:
+    def __init__(self, copies, place, piece):
+        self.k, self.g, self.piece = copies, place, piece
+        self.slots = copies.take(3)
+
+    def copy(self, rel):
+        piece = self.piece(self.g.d)
+        return self.k.to(piece, piece, (self.g.d ^ rel, self.g.c), self.slots + rel - 1)
+
+    def start(self):
+        for rel in (1, 2, 3):
+            self.copy(rel).start()
+
+    def finish(self):
+        for rel in (1, 2, 3):
+            self.copy(rel).wait_recv()
+
+    def drain(self):
+        for rel in (1, 2, 3):
+            self.copy(rel).wait_send()
+
+
+class Fold:
+    def __init__(self, copies, place, piece, got, stage):
+        self.k, self.g, self.piece, self.got, self.stage = copies, place, piece, got, stage
+        self.slots = copies.take(6)
+        self.loads = copies.take(6)
+
+    def first(self, half, passed):
+        g = self.g
+        rel = 1 + half
+        src = self.piece(g.d ^ (3 if passed else rel), half)
+        i = 2 * half + passed
+        return self.k.to(src, self.got(i), (g.d ^ rel, g.c), self.slots + i)
+
+    def second(self, half):
+        g = self.g
+        rel = 2 - half
+        return self.k.to(
+            self.piece(g.d ^ rel, half), self.got(4 + half), (g.d ^ rel, g.c), self.slots + 4 + half
+        )
+
+    def load(self, i):
+        return self.k.here(self.got(i), self.stage(i), self.loads + i)
+
+    def start(self):
+        for passed in (1, 0):
+            for half in range(2):
+                self.first(half, passed).start()
+
+    def middle(self, add):
+        for half in range(2):
+            self.first(half, 1).wait_recv()
+            self.load(2 * half + 1).start()
+        for half in range(2):
+            self.load(2 * half + 1).wait()
+            add(self.piece(self.g.d ^ (2 - half), half), (self.stage(2 * half + 1),))
+            self.second(half).start()
+
+    def final(self, add):
+        for half in range(2):
+            self.first(half, 0).wait_recv()
+            self.load(2 * half).start()
+        for half in range(2):
+            self.second(half).wait_recv()
+            self.load(4 + half).start()
+        for half in range(2):
+            self.load(2 * half).wait()
+            self.load(4 + half).wait()
+            add(self.piece(self.g.d, half), (self.stage(2 * half), self.stage(4 + half)))
+
+    def drain(self):
+        for half in range(2):
+            for passed in range(2):
+                self.first(half, passed).wait_send()
+            self.second(half).wait_send()
+
+
+def down_to_units(place, copies, src, dst):
+    g, p, d = place, place.p, place.d
+    send, receive = copies.take(8), copies.take(12)
+    odd = lax.rem(d, 2)
+    wide = (src.at[rows_at(p * 64, 128)], dst.at[rows_at(wide_row(p, d), 128)])
+    thin = (src.at[rows_at((1 - p) * 128, 64)], dst.at[rows_at(thin_row(d, p), 64)])
+    stays = odd == p
+
+    def thin_to(rel, core):
+        return copies.to(
+            *thin, (d ^ rel, 2 * g.z + odd), send + 4 + rel, receive + 4 + 2 * rel + core
+        )
+
+    def start_thin():
+        for rel in (1, 2, 3):
+            thin_to(rel, p).start()
+
+        @pl.when(stays)
+        def _():
+            copies.here(*thin, send + 4).start()
+
+        @pl.when(jnp.logical_not(stays))
+        def _():
+            thin_to(0, p).start()
+
+    copies.here(*wide, send).start()
+    spread = Spread(
+        copies, g, lambda e, half: dst.at[rows_at(wide_row(p, e) + half * 64, 64)]
+    )
+
+    def start_wide():
+        copies.here(*wide, send).wait()
+        spread.start()
+
+    def finish():
+        spread.finish()
+
+        @pl.when(stays)
+        def _():
+            copies.here(*thin, send + 4).wait()
+
+        @pl.when(jnp.logical_not(stays))
+        def _():
+            thin_to(0, p).wait_send()
+
+        for rel in (1, 2, 3):
+            thin_to(rel, p).wait_send()
+        for rel in range(4):
+
+            @pl.when(lax.rem(d ^ rel, 2) == p)
+            def _():
+                if rel:
+                    thin_to(rel, p).wait_recv()
+                thin_to(rel, 1 - p).wait_recv()
+
+    return start_thin, start_wide, spread, finish
+
+
+def unit_row(core, plane):
+    return (plane // 2) * 384 + (lax.rem(plane, 2) ^ core) * 256
+
+
+def wide_row(core, plane):
+    return unit_row(core, plane) + core * lax.rem(plane, 2) * 128
+
+
+def thin_row(plane, core):
+    odd = lax.rem(plane, 2)
+    return unit_row(odd, plane) + (1 - odd) * 128 + core * 64
+
+
+def down_to_owners(place, copies, src, dst):
+    g, p, d = place, place.p, place.d
+    send, receive = copies.take(12), copies.take(8)
+
+    def wide(rel):
+        plane = d ^ rel
+        a = src.at[rows_at(wide_row(p, plane), 128)]
+        b = dst.at[rel, rows_at(p * 64, 128)]
+        if rel == 0:
+            return copies.here(a, b, send)
+        return copies.to(a, b, (plane, g.c), send + rel, receive + rel)
+
+    def thin(rel, core):
+        plane = d ^ rel
+        a = src.at[rows_at(thin_row(plane, core), 64)]
+        b = dst.at[rel, rows_at((1 - core) * 128, 64)]
+        return copies.to(
+            a, b, (plane, 2 * g.z + core), send + 4 + 2 * rel + core, receive + 4 + rel
+        )
+
+    def thin_own():
+        a = src.at[rows_at(thin_row(d, p), 64)]
+        return copies.here(a, dst.at[0, rows_at((1 - p) * 128, 64)], send + 4 + p)
+
+    def holds(rel):
+        return lax.rem(d ^ rel, 2) == p
+
+    def start_wide():
+        for rel in (1, 2, 3, 0):
+            wide(rel).start()
+
+    def start_thin():
+        for rel in (1, 2, 3, 0):
+
+            @pl.when(holds(rel))
+            def _():
+                if rel:
+                    thin(rel, p).start()
+                else:
+                    thin_own().start()
+                thin(rel, 1 - p).start()
+
+    def finish():
+        wide(0).wait()
+        for rel in (1, 2, 3):
+            wide(rel).wait()
+        for rel in range(4):
+
+            @pl.when(holds(rel))
+            def _():
+                if rel:
+                    thin(rel, p).wait_send()
+                else:
+                    thin_own().wait()
+                thin(rel, 1 - p).wait_send()
+
+        @pl.when(jnp.logical_not(holds(0)))
+        def _():
+            thin(0, p).wait_recv()
+
+        for rel in (1, 2, 3):
+            thin(rel, p).wait_recv()
+
+    return start_wide, start_thin, finish
+
+
+UNIT_PARTS = ((0, 256), (256, 128), (384, 256), (640, 128))
+
+
+def unit_column(j, z, core):
+    plane = 2 * (j // 2) + (core if j % 2 == 0 else 1 - core)
+    return plane * 1536 + z * 384 + core * (128 if j % 2 == 0 else 256)
+
+
+def lanes(start, size):
+    return pl.ds(pl.multiple_of(start, 128), size)
+
+
+def nt(left, right):
+    return lax.dot_general(left, right, (((1,), (1,)), ((), ())), preferred_element_type=F32)
+
+
+def tn(left, right):
+    return lax.dot_general(left, right, (((0,), (0,)), ((), ())), preferred_element_type=F32)
+
+
+def layer_kernel(
+    x, prefix, wq, wk, wv, wo, wg, wu, wd, gains, cosine, sine, dy,
+    output, x_grad, gain_out, out_q, out_k, out_v, out_o, out_g, out_u, out_d,
+    n1_kept, got_gu, got_d, got_qkv,
+    xs, n1, ys, partial, partial2, from_twin, from_left, from_right, from_twin2, from_left2, from_right2,
+    w_qkv, w_o, w_gu, w_d, qkv, raw, o, lse, act, d_gu, hidden, d_hidden, x_own, d_kv, d_qkv,
+    wo_mid, wo_back, got_o, gain_buf, gain_acc, gain_one, gain_two, gain_qk, gain_vec, gain_ctx, gain_dp,
+    sends, receives,
+):
+    g = Place()
+    k = Copies(sends, receives)
+    d, c, z, p = g.d, g.c, g.z, g.p
+    meet()
+    own = rows_at(c * BLOCK, BLOCK)
+    shard = rows_at(d * 512, 512)
+    mine = rows_at(d * 512 + c * 64, 64)
+
+    gain_buf[d, c] = gains[...]
+    gain_slots = k.take(12)
+
+    def gain_over_ctx(rel):
+        return k.to(gain_buf.at[d, c], gain_buf.at[d, c], (d, c ^ rel), gain_slots + rel)
+
+    def gain_over_dp(rel):
+        return k.to(gain_buf.at[d], gain_buf.at[d], (d ^ rel, c), gain_slots + 8 + rel)
+
+    for rel in range(1, 8):
+        gain_over_ctx(rel).start()
+
+    own_slots = k.take(3)
+    own_copies = [
+        k.here(x, xs.at[own], own_slots),
+        k.here(x, x_own, own_slots + 1),
+        k.here(dy, ys.at[own], own_slots + 2),
+    ]
+    for copy in own_copies:
+        copy.start()
+
+    qkv_slots = k.take(24)
+
+    def qkv_to(rel, j):
+        other = c ^ rel
+        width = 256 if j == 0 else 128
+        src = (wq, wk, wv)[j].at[:, lanes(other * width, width)]
+        dst = w_qkv.at[mine, pl.ds((0, 256, 384)[j], width)]
+        slot = qkv_slots + 3 * rel + j
+        return k.to(src, dst, (d, other), slot) if rel else k.here(src, dst, slot)
+
+    for rel in range(8):
+        for j in range(3):
+            qkv_to(rel, j).start()
+    own_copies[0].wait()
+    tokens = Gather(k, g, xs)
+    tokens.start()
+    at_end = (z == 0) | (z == 3)
+    gu_slots = k.take(64)
+
+    def gu_to(which, rel, j):
+        place, count = UNIT_PARTS[j]
+        column = unit_column(j, z ^ (rel // 2), p ^ (rel % 2))
+        src = (wg, wu)[which].at[:, lanes(column, count)]
+        dst = w_gu.at[mine, pl.ds(which * 768 + place, count)]
+        slot = gu_slots + which * 32 + rel * 4 + j
+        return k.to(src, dst, (d, c ^ rel), slot) if rel else k.here(src, dst, slot)
+
+    def gu_start(*groups):
+        for which in range(2):
+            for group in groups:
+                for rel in (2 * group, 2 * group + 1):
+                    for j in range(4):
+                        gu_to(which, rel, j).start()
+
+    @pl.when(at_end)
+    def _():
+        gu_start(1)
+
+
+    wo_slots = k.take(20)
+    far = c // 4
+
+    def wo_over_dp(rel):
+        src, dst = wo.at[rows_at((d ^ rel) * 16, 16)], wo_mid.at[d]
+        slot = wo_slots + rel
+        return k.to(src, dst, (d ^ rel, c), slot) if rel else k.here(src, dst, slot)
+
+    def wo_over_ctx(rel):
+        src, dst = wo_mid.at[z ^ rel], w_o.at[lax.rem(c, 4), rows_at(d * 16, 16)]
+        return k.to(
+            src, dst, (d, 2 * (z ^ rel) + far), wo_slots + 4 + rel, wo_slots + 8 + lax.rem(c, 4)
+        )
+
+    def wo_stay():
+        return k.here(
+            wo_mid.at[z], w_o.at[lax.rem(c, 4), rows_at(d * 16, 16)], wo_slots + 4
+        )
+
+    wo_stays = far == p
+    for rel in range(4):
+        wo_over_dp(rel).start()
+
+    start_thin, start_wide, spread_wide, finish_down = down_to_units(g, k, wd, w_d)
+
+    for rel in range(1, 8):
+        gain_over_ctx(rel).wait_recv()
+    for rel in range(1, 4):
+        gain_over_dp(rel).start()
+    start_thin()
+    for rel in range(1, 4):
+        gain_over_dp(rel).wait_recv()
+    gain_acc[...] = jnp.zeros_like(gain_acc)
+    for i in range(32):
+        row = gain_buf[i // 8, i % 8][0:8, :].astype(F32)
+        row = jnp.concatenate([row, jnp.zeros((8, 128), F32)], 1)
+        shift = (8 * i) % 128
+        if shift:
+            row = pltpu.roll(row, shift, 1)
+        first = 136 * i - shift
+        gain_acc[:, first : first + 384] += row
+
+    def normalize(block):
+        def body(i, carry):
+            at = rows_at(block * BLOCK + i * 16, 16)
+            v = xs[at, :].astype(F32)
+            r = lax.rsqrt(jnp.mean(v * v, -1, keepdims=True) + EPSILON)
+            n1[at, :] = (v * r * gain_acc[0:1, 0:2048]).astype(BF)
+            return carry
+
+        lax.fori_loop(0, BLOCK // 16, body, 0)
+
+    normalize(c)
+    for j in range(3):
+        qkv_to(0, j).wait()
+        for rel in range(1, 8):
+            qkv_to(rel, j).wait_recv()
+    spread_qkv = Spread(k, g, lambda e, half: w_qkv.at[rows_at(e * 512 + half * 256, 256)])
+    spread_qkv.start()
+    tokens.twin_own()
+    normalize(c ^ 1)
+
+    def each_side(step, use):
+        def side(i, carry):
+            chip = jnp.where(i == 0, z - 1 - step, z + 1 + step)
+
+            @pl.when((chip >= 0) & (chip <= 3))
+            def _():
+                use(chip)
+
+            return carry
+
+        lax.fori_loop(0, 2, side, 0)
+
+    def normalize_chip(chip):
+        normalize(2 * chip)
+        normalize(2 * chip + 1)
+
+    gain_q, gain_k = gain_acc[0:1, 4096:4224], gain_acc[0:1, 4224:4352]
+
+    def rotated(value, gain, at):
+        r = lax.rsqrt(jnp.mean(value * value, -1, keepdims=True) + EPSILON)
+        value = value * r * gain
+        return value * cosine[at, :] + pltpu.roll(value, 64, 1) * sine[at, :]
+
+    def project(chip):
+        at = rows_at(chip * 256, 256)
+        product = jnp.dot(n1[at, :], w_qkv[...], preferred_element_type=F32)
+        raw[at, :] = product[:, :384]
+        for j, gain in ((0, gain_q), (1, gain_q), (2, gain_k)):
+            qkv[at, j * 128 : j * 128 + 128] = rotated(
+                product[:, j * 128 : j * 128 + 128], gain, at
+            ).astype(BF)
+        qkv[at, 384:512] = product[:, 384:].astype(BF)
+
+    def project_all(first, last):
+        def body(i, carry):
+            step = first + i // 2
+            chip = jnp.where(lax.rem(i, 2) == 0, z - 1 - step, z + 1 + step)
+
+            @pl.when((chip >= 0) & (chip <= 3) & ((step >= 0) | (lax.rem(i, 2) == 0)))
+            def _():
+                project(chip)
+
+            return carry
+
+        lax.fori_loop(0, 2 * (last - first), body, 0)
+
+    tokens.step(0)
+
+    @pl.when(jnp.logical_not(at_end))
+    def _():
+        gu_start(3)
+
+    for rel in range(4):
+        if rel == 0:
+            wo_over_dp(0).wait()
+        else:
+            wo_over_dp(rel).wait_recv()
+    for rel in range(1, 4):
+        wo_over_ctx(rel).start()
+
+    @pl.when(wo_stays)
+    def _():
+        wo_stay().start()
+
+    @pl.when(jnp.logical_not(wo_stays))
+    def _():
+        wo_over_ctx(0).start()
+
+    tokens.twin_step(0)
+    each_side(0, normalize_chip)
+    tokens.step(1)
+    spread_qkv.forward()
+    tokens.twin_step(1)
+    each_side(1, normalize_chip)
+    for i in range(4):
+
+        @pl.when(jnp.logical_not(c == 4 * p + i))
+        def _():
+            src, dst = wo_mid.at[0], w_o.at[0, rows_at(0, 16)]
+            k.to(src, dst, (d, c ^ 1), wo_slots + 4, wo_slots + 8 + i).wait_recv()
+
+    @pl.when(wo_stays)
+    def _():
+        wo_stay().wait()
+
+    spread_o = Direct(k, g, lambda e: w_o.at[:, rows_at(e * 16, 16)])
+    spread_o.start()
+    start_wide()
+    spread_qkv.finish()
+    project_all(-1, 1)
+    tokens.step(2)
+    tokens.twin_step(2)
+    each_side(2, normalize_chip)
+
+    def gu_take(which):
+        for rel in range(8):
+            for j in range(4):
+                if rel == 0:
+                    gu_to(which, rel, j).wait()
+                else:
+                    gu_to(which, rel, j).wait_recv()
+
+    @pl.when(at_end)
+    def _():
+        gu_start(0, 2, 3)
+
+    project_all(1, 3)
+    keep_slots = k.take(2)
+    keep = k.here(n1, n1_kept, keep_slots)
+    keep.start()
+
+    limit = prefix[0]
+    scale = HEAD_SIZE**-0.5
+
+    def head_scores(head, at, first_row):
+        scores = nt(qkv[at, head * 128 : head * 128 + 128], qkv[:, 256:384]) * scale
+        row = first_row + lax.broadcasted_iota(jnp.int32, (256, 1), 0)
+        column = lax.broadcasted_iota(jnp.int32, (1, 1024), 1)
+        return jnp.where(column < jnp.maximum(row + 1, limit), scores, -1e30)
+
+    def attend(head):
+        def body(i, carry):
+            at = rows_at(i * 256, 256)
+            scores = head_scores(head, at, i * 256)
+            top = jnp.max(scores, -1, keepdims=True)
+            expo = jnp.exp(scores - top)
+            total = jnp.sum(expo, -1, keepdims=True)
+            probs = (expo * (1.0 / total)).astype(BF)
+            value = jnp.dot(probs, qkv[:, 384:512], preferred_element_type=F32)
+            o[at, head * 128 : head * 128 + 128] = value.astype(BF)
+            lse[head, at, :] = jnp.broadcast_to(top + jnp.log(total), (256, 128))
+            return carry
+
+        lax.fori_loop(0, 4, body, 0)
+
+    attend(0)
+    attend(1)
+
+    @pl.when(jnp.logical_not(at_end))
+    def _():
+        gu_start(0, 1, 2)
+
+    spread_wide.forward()
+    tokens.drain()
+    spread_o.finish()
+    sum_one = Scatter(k, g, partial, from_twin, from_left, from_right)
+    for chip in (3, 0, 2, 1):
+
+        def columns(j, carry):
+            cols = lanes(j * 512, 512)
+            rows = pl.ds(chip * 256, 256)
+            value = jnp.dot(
+                o[rows, :], w_o[:, :, cols].reshape(256, 512), preferred_element_type=F32
+            )
+            partial[rows, cols] = value.astype(BF)
+            return carry
+
+        lax.fori_loop(0, 4, columns, 0)
+        sum_one.send_twin(chip)
+    own_copies[2].wait()
+    d_hidden[...] = ys[own, :].astype(F32)
+    upstream = Gather(k, g, ys)
+
+    def upstream_goes(step):
+        upstream.start_line(step == z, step == 3 - z)
+
+
+    sum_one.take_twin(3)
+    sum_one.take_twin(0)
+    sum_one.send_ends(0, 0)
+    sum_one.take_twin(2)
+    sum_one.take_twin(1)
+    sum_one.send_ends(0, 1, 2)
+    sum_one.send_ends(1, 0, 1, 2)
+    gu_take(0)
+    spread_gate = Spread(
+        k, g, lambda e, half: w_gu.at[rows_at(e * 512 + half * 256, 256), pl.ds(0, 768)]
+    )
+    spread_gate.start()
+    sum_one.relay(0, 0)
+    gu_take(1)
+    spread_up = Spread(
+        k, g, lambda e, half: w_gu.at[rows_at(e * 512 + half * 256, 256), pl.ds(768, 768)]
+    )
+    spread_up.start()
+    sum_one.relay(1, 0)
+    own_copies[1].wait()
+
+    def done_one(at, value):
+        rows = rows_at(at, 16)
+        h = x_own[rows, :].astype(F32) + value
+        r = lax.rsqrt(jnp.mean(h * h, -1, keepdims=True) + EPSILON)
+        hidden[rows, :] = h
+        xs[rows_at(c * BLOCK + at, 16), :] = (h * r * gain_acc[0:1, 2048:4096]).astype(BF)
+
+    seconds = Gather(k, g, xs)
+    sum_one.last(done_one, 0)
+    seconds.start_part(0)
+    sum_one.relay(0, 1)
+    spread_gate.forward()
+    sum_one.relay(1, 1)
+    seconds.step_part(0, 0)
+    sum_one.last(done_one, 1)
+    seconds.start_part(1)
+    spread_up.forward()
+    upstream_goes(0)
+    upstream.start_twin()
+    seconds.step_part(1, 0)
+    seconds.step_part(0, 1)
+    upstream_goes(1)
+    spread_gate.finish()
+    finish_down()
+    sum_one.drain()
+    keep.wait()
+    spread_up.finish()
+    sum_two = Scatter(k, g, partial2, from_twin, from_left, from_right)
+    sum_out = Scatter(k, g, partial, from_twin2, from_left2, from_right2, parts=1)
+
+    def feed_forward(chip):
+        at = rows_at(chip * 256, 256)
+
+        def units(j, carry):
+            cols, up_cols = lanes(j * 256, 256), lanes(768 + j * 256, 256)
+            gate = jnp.dot(xs[at, :], w_gu[:, cols], preferred_element_type=F32)
+            up = jnp.dot(xs[at, :], w_gu[:, up_cols], preferred_element_type=F32)
+            act[at, cols] = (gate * up * (1.0 / (1.0 + jnp.exp(-gate)))).astype(BF)
+            d_gu[at, cols] = gate.astype(BF)
+            d_gu[at, up_cols] = up.astype(BF)
+            return carry
+
+        lax.fori_loop(0, 3, units, 0)
+
+        def columns(j, carry):
+            cols = lanes(j * 512, 512)
+            partial[at, cols] = jnp.dot(
+                act[at, :], w_d[:, cols], preferred_element_type=F32
+            ).astype(BF)
+            return carry
+
+        lax.fori_loop(0, 4, columns, 0)
+        sum_out.send_twin(chip)
+
+    def feed_back(chip):
+        at = rows_at(chip * 256, 256)
+
+        def units(j, carry):
+            cols, up_cols = lanes(j * 256, 256), lanes(768 + j * 256, 256)
+            d_act = nt(ys[at, :], w_d[rows_at(j * 256, 256), :])
+            gate, up = d_gu[at, cols].astype(F32), d_gu[at, up_cols].astype(F32)
+            sig = 1.0 / (1.0 + jnp.exp(-gate))
+            d_gu[at, cols] = (d_act * up * sig * (1.0 + gate * (1.0 - sig))).astype(BF)
+            d_gu[at, up_cols] = (d_act * gate * sig).astype(BF)
+            return carry
+
+        lax.fori_loop(0, 3, units, 0)
+
+        def columns(j, carry):
+            rows = rows_at(j * 512, 512)
+            partial2[at, lanes(j * 512, 512)] = nt(d_gu[at, :], w_gu[rows, :]).astype(BF)
+            return carry
+
+        lax.fori_loop(0, 4, columns, 0)
+        sum_two.send_twin(chip)
+
+    def visit(gather, use, between=None, taken=(0, 0), used=None):
+        inner = jnp.where(z <= 1, 1, -1)
+
+        def body(step, carry):
+            @pl.when(step == 0)
+            def _():
+                gather.twin_own()
+
+            @pl.when(step > 0)
+            @jax.named_scope("twin")
+            def _():
+                gather.twin_step(step - 1)
+
+            def side(i, carry):
+                chip = jnp.where(i == 0, z + inner * step, z - inner * step)
+
+                @pl.when((chip >= 0) & (chip <= 3) & ((i == 0) | (step > 0)))
+                @jax.named_scope("use")
+                def _():
+                    use(chip)
+
+                if used is not None:
+
+                    @pl.when(i == 0)
+                    def _():
+                        used(step)
+
+                for part in range(gather.parts):
+
+                    @pl.when((i == 0) & (step >= taken[part]) & (step < 3))
+                    @jax.named_scope("arrive")
+                    def _():
+                        gather.step_part(step, part)
+
+                if between is not None:
+
+                    @pl.when(i == 0)
+                    @jax.named_scope("between")
+                    def _():
+                        between(step)
+
+                return carry
+
+            lax.fori_loop(0, 2, side, 0)
+            return carry
+
+        lax.fori_loop(0, 4, body, 0)
+
+    def upstream_passes(step):
+        @pl.when(step == 1)
+        def _():
+            upstream_goes(2)
+
+        @pl.when((step == 2) & jnp.logical_not(at_end))
+        def _():
+            upstream.step(0)
+
+    visit(seconds, feed_forward, taken=(2, 1), between=upstream_passes)
+
+    @pl.when(at_end)
+    def _():
+        upstream.step(0)
+
+    for i in (3, 0):
+        sum_out.take_twin(i)
+    sum_out.start()
+    for i in (2, 1):
+        sum_out.take_twin(i)
+
+    @pl.when(at_end)
+    def _():
+        sum_out.advance(0)
+
+    def out_goes(step):
+        @pl.when((step == 3) & jnp.logical_not(at_end))
+        def _():
+            sum_out.advance(0)
+
+    visit(upstream, feed_back, taken=(1, 1), between=out_goes)
+    sum_two.take_twin(3)
+    sum_two.take_twin(0)
+    sum_two.send_ends(0, 0)
+    sum_two.take_twin(2)
+    sum_two.take_twin(1)
+    sum_two.send_ends(0, 1, 2)
+    sum_two.send_ends(1, 0, 1)
+    for spread in (spread_qkv, spread_o, spread_wide, spread_gate, spread_up):
+        spread.drain()
+    upstream.drain()
+    seconds.drain()
+
+    def fold_gu(which):
+        cols = pl.ds(which * 768, 768)
+
+        def stage(i):
+            block = (0, 4, 1, 5, 2, 3)[i]
+            return ys.at[pl.ds((block // 2) * 256, 256), pl.ds((block % 2) * 768, 768)]
+
+        return Fold(
+            k, g, lambda e, half: w_gu.at[rows_at(e * 512 + half * 256, 256), cols],
+            lambda i: got_gu.at[i, :, cols], stage,
+        )
+
+    folds = [fold_gu(0), fold_gu(1)]
+
+    def add_stages(piece, stages):
+        def body(i, carry):
+            rows = pl.ds(pl.multiple_of(i * 16, 16), 16)
+            value = piece[rows, :].astype(F32)
+            for stage in stages:
+                value = value + stage[rows, :].astype(F32)
+            piece[rows, :] = value.astype(BF)
+            return carry
+
+        lax.fori_loop(0, 16, body, 0)
+
+    def gu_gradient(which):
+        def body(j, carry):
+            cols = lanes(j * 512, 512)
+            w_gu[rows_at(j * 512, 512), which * 768 : which * 768 + 768] = tn(
+                xs[:, cols], d_gu[:, which * 768 : which * 768 + 768]
+            ).astype(BF)
+            return carry
+
+        lax.fori_loop(0, 4, body, 0)
+        folds[which].start()
+
+    def down_gradient(j, carry):
+        rows = rows_at(j * 256, 256)
+        for i in range(2):
+            cols = slice(i * 1024, i * 1024 + 1024)
+            w_d[rows, cols] = tn(act[:, lanes(j * 256, 256)], ys[:, cols]).astype(BF)
+        return carry
+
+    gu_gradient(0)
+    gu_gradient(1)
+    load = k.here(n1_kept, xs, keep_slots + 1)
+    load.start()
+    lax.fori_loop(0, 3, down_gradient, 0)
+    start_wide_back, start_thin_back, finish_down_back = down_to_owners(g, k, w_d, got_d)
+    start_wide_back()
+    sum_two.relay(0, 0)
+    folds[0].middle(add_stages)
+    sum_two.relay(1, 0)
+    gain_two[...] = jnp.zeros_like(gain_two)
+
+    def done_two(at, value):
+        rows = rows_at(at, 16)
+        there = rows_at(c * BLOCK + at, 16)
+        h = hidden[rows, :]
+        r = lax.rsqrt(jnp.mean(h * h, -1, keepdims=True) + EPSILON)
+        scaled = value * gain_acc[0:1, 2048:4096]
+        mean = jnp.mean(h * scaled, -1, keepdims=True)
+        d_h = d_hidden[rows, :] + r * scaled - h * (r * r * r * mean)
+        part = value * h * r
+        gain_two[...] += part[0:8, :] + part[8:16, :]
+        d_hidden[rows, :] = d_h
+        n1[there, :] = d_h.astype(BF)
+
+    thirds = Gather(k, g, n1)
+    sum_two.last(done_two, 0)
+    thirds.start_part(0)
+    sum_two.send_ends(1, 2)
+
+    @pl.when(at_end)
+    def _():
+        sum_out.advance(1)
+
+    sum_two.relay(0, 1)
+    sum_two.relay(1, 1)
+    thirds.step_part(0, 0)
+    sum_two.last(done_two, 1)
+    thirds.start_part(1)
+
+    folds[1].middle(add_stages)
+    thirds.step_part(1, 0)
+    thirds.step_part(0, 1)
+
+    sum_two.drain()
+    d_kv[...] = jnp.zeros_like(d_kv)
+    gain_qk[...] = jnp.zeros_like(gain_qk)
+
+    def unrotated(gradient, value, gain, at):
+        gradient = gradient * cosine[at, :] + pltpu.roll(gradient * sine[at, :], 64, 1)
+        r = lax.rsqrt(jnp.mean(value * value, -1, keepdims=True) + EPSILON)
+        part = gradient * value * r
+        gradient = gradient * gain
+        mean = jnp.mean(gradient * value, -1, keepdims=True)
+        result = gradient * r - value * (r * r * r * mean)
+        return result, jnp.sum(part.reshape(-1, 8, 128), 0)
+
+    def attend_back(chip):
+        at = rows_at(chip * 256, 256)
+        d_o = nt(n1[at, :], w_o[...].reshape(256, 2048)).astype(BF)
+        for head in range(2):
+            cols = slice(head * 128, head * 128 + 128)
+            probs = jnp.exp(head_scores(head, at, chip * 256) - lse[head, at, 0:1])
+            d_probs = nt(d_o[:, cols], qkv[:, 384:512])
+            delta = jnp.sum(d_probs * probs, -1, keepdims=True)
+            d_scores = (probs * (d_probs - delta)).astype(BF)
+            d_q = jnp.dot(d_scores, qkv[:, 256:384], preferred_element_type=F32) * scale
+            d_kv[:, 0:128] += tn(d_scores, qkv[at, cols]) * scale
+            d_kv[:, 128:256] += tn(probs.astype(BF), d_o[:, cols])
+            d_q, part = unrotated(d_q, raw[at, cols], gain_q, at)
+            d_qkv[at, cols] = d_q.astype(BF)
+            gain_qk[:, 0:128] += part
+
+    stage_slots = k.take(16)
+    gu_back = k.take(64)
+
+    def gu_home(which, rel, j):
+        place, count = UNIT_PARTS[j]
+        src = w_gu.at[rows_at(d * 512 + (c ^ rel) * 64, 64), pl.ds(which * 768 + place, count)]
+        dst = (out_g, out_u)[which].at[:, lanes(unit_column(j, z, p), count)]
+        slot = gu_back + which * 32 + rel * 4 + j
+        return k.to(src, dst, (d, c ^ rel), slot) if rel else k.here(src, dst, slot)
+
+    def sum_gu(which):
+        folds[which].final(add_stages)
+        for rel in range(8):
+            for j in range(4):
+                gu_home(which, rel, j).start()
+
+    def meanwhile(step):
+        @pl.when(step == 1)
+        def _():
+            @pl.when(jnp.logical_not(at_end))
+            def _():
+                sum_out.advance(1)
+
+            sum_gu(0)
+
+        @pl.when(step == 2)
+        def _():
+            sum_gu(1)
+
+    visit(thirds, attend_back, taken=(2, 1), between=meanwhile)
+
+    attn_slots = k.take(8)
+
+    def qkv_rows(e, first, count):
+        return d_gu.at[rows_at(lax.rem(e, 2) * 512 + first, count), lanes((e // 2) * 512, 512)]
+
+    def qkv_over_dp(rel):
+        return k.to(
+            qkv_rows(d ^ rel, 0, 512), got_qkv.at[rel - 1], (d ^ rel, c), attn_slots + rel - 1
+        )
+
+    def wo_grad_over_dp(rel):
+        src = w_o.at[:, rows_at((d ^ rel) * 16, 16)]
+        return k.to(src, got_o.at[rel - 1], (d ^ rel, c), attn_slots + 3 + rel)
+
+    def wo_gradient(j, carry):
+        cols = lanes(j * 512, 512)
+        w_o[:, :, cols] = tn(o[...], n1[:, cols]).astype(BF).reshape(4, 64, 512)
+        return carry
+
+    lax.fori_loop(0, 4, wo_gradient, 0)
+    for rel in (1, 2, 3):
+        wo_grad_over_dp(rel).start()
+
+    def finish_keys(i, carry):
+        at = rows_at(i * 256, 256)
+        d_k, part = unrotated(d_kv[at, 0:128], raw[at, 256:384], gain_k, at)
+        d_qkv[at, 256:384] = d_k.astype(BF)
+        d_qkv[at, 384:512] = d_kv[at, 128:256].astype(BF)
+        gain_qk[:, 128:256] += part
+        return carry
+
+    lax.fori_loop(0, 4, finish_keys, 0)
+    load.wait()
+
+    def qkv_gradient(e, carry):
+        cols = lanes(e * 512, 512)
+        rows, place = rows_at(lax.rem(e, 2) * 512, 512), lanes((e // 2) * 512, 512)
+        d_gu[rows, place] = tn(xs[:, cols], d_qkv[...]).astype(BF)
+        return carry
+
+    lax.fori_loop(0, 4, qkv_gradient, 0)
+    for rel in (1, 2, 3):
+        qkv_over_dp(rel).start()
+    start_thin_back()
+    sum_three = Scatter(k, g, partial2, from_twin, from_left, from_right)
+    for chip in (3, 0, 2, 1):
+
+        def columns(j, carry):
+            cols = lanes(j * 512, 512)
+            rows = pl.ds(chip * 256, 256)
+            value = nt(d_qkv[rows, :], w_qkv[rows_at(j * 512, 512), :])
+            partial2[rows, cols] = value.astype(BF)
+            return carry
+
+        lax.fori_loop(0, 4, columns, 0)
+        sum_three.send_twin(chip)
+    sum_three.take_twin(3)
+    sum_three.take_twin(0)
+    sum_three.start()
+    sum_three.take_twin(2)
+    sum_three.take_twin(1)
+
+    def gain_columns(e, carry):
+        rows, place = rows_at(lax.rem(e, 2) * 512, 512), lanes((e // 2) * 512, 512)
+        product = d_gu[rows, place].astype(F32) * w_qkv[rows_at(e * 512, 512), :].astype(F32)
+        gain_one[:, lanes(e * 512, 512)] = nt(jnp.ones((8, 512), BF), product.astype(BF))
+        return carry
+
+    lax.fori_loop(0, 4, gain_columns, 0)
+    gain_vec[:, 0:2048] = gain_one[0:1, :] / gain_acc[0:1, 0:2048]
+    gain_vec[:, 2048:4096] = jnp.sum(gain_two[...], 0, keepdims=True)
+    gain_vec[:, 4096:4352] = jnp.sum(gain_qk[...], 0, keepdims=True)
+    sum_slots = k.take(12)
+
+    def gain_sum_over_ctx(rel):
+        return k.to(gain_vec, gain_ctx.at[rel - 1], (d, c ^ rel), sum_slots + rel)
+
+    def gain_sum_over_dp(rel):
+        return k.to(gain_out, gain_dp.at[rel - 1], (d ^ rel, c), sum_slots + 8 + rel)
+
+    for rel in range(1, 8):
+        gain_sum_over_ctx(rel).start()
+    for rel in (1, 2, 3):
+        wo_grad_over_dp(rel).wait()
+    for i in range(4):
+        rows = rows_at(d * 16, 16)
+        value = w_o[i, rows, :].astype(F32)
+        for j in range(3):
+            value = value + got_o[j, i].astype(F32)
+        w_o[i, rows, :] = value.astype(BF)
+    back_slots = k.take(20)
+
+    def wo_back_ctx(i):
+        src, dst = w_o.at[i, rows_at(d * 16, 16)], wo_back.at[z]
+        return k.to(src, dst, (d, 4 * p + i), back_slots + i, back_slots + 4 + z)
+
+    def wo_back_here(i):
+        return k.here(w_o.at[i, rows_at(d * 16, 16)], wo_back.at[z], back_slots + i)
+
+    def wo_home(rel):
+        src, dst = wo_back.at[d ^ rel], out_o.at[rows_at(d * 16, 16)]
+        slot = back_slots + 8 + rel
+        return k.to(src, dst, (d ^ rel, c), slot) if rel else k.here(src, dst, slot)
+
+    for i in range(4):
+
+        @pl.when(c == 4 * p + i)
+        def _():
+            wo_back_here(i).start()
+
+        @pl.when(c != 4 * p + i)
+        def _():
+            wo_back_ctx(i).start()
+
+    sum_three.advance(0)
+
+
+    sum_three.advance(1)
+
+    qkv_back = k.take(24)
+
+    def qkv_home(rel, j):
+        other = c ^ rel
+        width = 256 if j == 0 else 128
+        src = d_gu.at[
+            rows_at(lax.rem(d, 2) * 512 + other * 64, 64),
+            lanes((d // 2) * 512 + (0, 256, 384)[j], width),
+        ]
+        dst = (out_q, out_k, out_v)[j].at[:, lanes(c * width, width)]
+        slot = qkv_back + 3 * rel + j
+        return k.to(src, dst, (d, other), slot) if rel else k.here(src, dst, slot)
+
+    for rel in (1, 2, 3):
+        qkv_over_dp(rel).wait()
+    qkv_stage = [
+        k.here(
+            got_qkv.at[i],
+            ys.at[pl.ds(512, 512), pl.ds(i * 512, 512)],
+            stage_slots + 11 + i,
+        )
+        for i in range(3)
+    ]
+    for copy in qkv_stage:
+        copy.start()
+    for copy in qkv_stage:
+        copy.wait()
+
+    def add_qkv(i, carry):
+        at = i * 16
+        rows, place = rows_at(lax.rem(d, 2) * 512 + at, 16), lanes((d // 2) * 512, 512)
+        value = d_gu[rows, place].astype(F32)
+        for j in range(3):
+            value = value + ys[rows_at(512 + at, 16), j * 512 : j * 512 + 512].astype(F32)
+        d_gu[rows, place] = value.astype(BF)
+        return carry
+
+    lax.fori_loop(0, 32, add_qkv, 0)
+    for rel in range(8):
+        for j in range(3):
+            qkv_home(rel, j).start()
+    for j in range(4):
+
+        @pl.when(jnp.logical_not((j == z) & wo_stays))
+        def _():
+            src, dst = w_o.at[0, rows_at(0, 16)], wo_back.at[0]
+            k.to(src, dst, (d, c ^ 1), back_slots, back_slots + 4 + j).wait_recv()
+
+    for i in range(4):
+
+        @pl.when(c == 4 * p + i)
+        def _():
+            wo_back_here(i).wait()
+
+        @pl.when(c != 4 * p + i)
+        def _():
+            wo_back_ctx(i).wait_send()
+
+    for rel in range(4):
+        wo_home(rel).start()
+
+    total = gain_vec[...]
+    for rel in range(1, 8):
+        gain_sum_over_ctx(rel).wait()
+        total = total + gain_ctx[rel - 1]
+    gain_out[...] = total
+    for rel in range(1, 4):
+        gain_sum_over_dp(rel).start()
+
+    sum_out.advance(2)
+
+    def done_out(at, value):
+        rows = rows_at(at, 16)
+        output[rows, :] = (hidden[rows, :] + value).astype(BF)
+
+    sum_out.finish(done_out)
+
+    finish_down_back()
+    stages = [
+        k.here(got_d.at[i], ys.at[pl.ds(i * 192, 192)], stage_slots + 6 + i) for i in range(4)
+    ]
+    for copy in stages:
+        copy.start()
+    for copy in stages:
+        copy.wait()
+
+    def add_down(i, carry):
+        at = i * 16
+        value = 0.0
+        for j in range(4):
+            value = value + ys[rows_at(j * 192 + at, 16), :].astype(F32)
+        ys[rows_at(at, 16), :] = value.astype(BF)
+        return carry
+
+    lax.fori_loop(0, 12, add_down, 0)
+    down_home = k.here(ys.at[pl.ds(0, 192)], out_d, stage_slots + 10)
+    down_home.start()
+
+    sum_three.advance(2)
+
+    def done_three(at, value):
+        rows = rows_at(at, 16)
+        v = x_own[rows, :].astype(F32)
+        r = lax.rsqrt(jnp.mean(v * v, -1, keepdims=True) + EPSILON)
+        scaled = value * gain_acc[0:1, 0:2048]
+        mean = jnp.mean(v * scaled, -1, keepdims=True)
+        x_grad[rows, :] = (d_hidden[rows, :] + r * scaled - v * (r * r * r * mean)).astype(BF)
+
+    sum_three.finish(done_three)
+    total = gain_out[...]
+    for rel in range(1, 4):
+        gain_sum_over_dp(rel).wait()
+        total = total + gain_dp[rel - 1]
+    gain_out[...] = total
+
+    for rel in range(8):
+        for j in range(3):
+            qkv_home(rel, j).wait()
+            if rel:
+                qkv_to(rel, j).wait_send()
+        for which in range(2):
+            for j in range(4):
+                gu_home(which, rel, j).wait()
+                if rel:
+                    gu_to(which, rel, j).wait_send()
+        if rel:
+            gain_over_ctx(rel).wait_send()
+    for rel in range(4):
+        wo_home(rel).wait()
+        if rel:
+            gain_over_dp(rel).wait_send()
+            wo_over_dp(rel).wait_send()
+            wo_over_ctx(rel).wait_send()
+
+    @pl.when(jnp.logical_not(wo_stays))
+    def _():
+        wo_over_ctx(0).wait_send()
+
+    down_home.wait()
+    for fold in folds:
+        fold.drain()
+    thirds.drain()
+    sum_out.drain()
+    sum_three.drain()
+
+
+def run_layer(x, prefix, wq, wk, wv, wo, wg, wu, wd, gains, cosine, sine, dy):
+    width = 2048
+    any_space, vmem = pl.BlockSpec(memory_space=pl.ANY), pl.BlockSpec(memory_space=pltpu.VMEM)
+    shape, hold = jax.ShapeDtypeStruct, pltpu.VMEM
+    return pl.pallas_call(
+        layer_kernel,
+        out_shape=(
+            shape((BLOCK, width), BF), shape((BLOCK, width), BF), shape((1, 4352), F32),
+            shape((64, 2048), BF), shape((64, 1024), BF), shape((64, 1024), BF), shape((64, 2048), BF),
+            shape((64, 6144), BF), shape((64, 6144), BF), shape((192, 2048), BF),
+            shape((1024, width), BF), shape((6, 256, 1536), BF), shape((4, 192, 2048), BF),
+            shape((3, 512, 512), BF),
+        ),
+        in_specs=[any_space, pl.BlockSpec(memory_space=pltpu.SMEM)] + [any_space] * 7 + [vmem] * 3 + [any_space],
+        out_specs=(vmem,) * 3 + (any_space,) * 11,
+        scratch_shapes=[
+            hold((1024, width), BF), hold((1024, width), BF), hold((1024, width), BF),
+            hold((1024, width), BF), hold((1024, width), BF),
+            hold((512, width), BF), hold((384, width), BF), hold((384, width), BF),
+            hold((512, width), BF), hold((384, width), BF), hold((384, width), BF),
+            hold((width, 512), BF), hold((4, 64, width), BF), hold((width, 1536), BF), hold((768, width), BF),
+            hold((1024, 512), BF), hold((1024, 384), F32), hold((1024, 256), BF), hold((2, 1024, 128), F32),
+            hold((1024, 768), BF), hold((1024, 1536), BF),
+            hold((BLOCK, width), F32), hold((BLOCK, width), F32), hold((BLOCK, width), BF),
+            hold((1024, 256), F32), hold((1024, 512), BF),
+            hold((4, 16, width), BF), hold((4, 16, width), BF), hold((3, 4, 16, width), BF),
+            hold((4, 8, 16, 256), BF), hold((8, 4608), F32), hold((8, width), F32), hold((8, width), F32),
+            hold((8, 256), F32), hold((1, 4352), F32), hold((7, 1, 4352), F32), hold((3, 1, 4352), F32),
+            pltpu.SemaphoreType.DMA((SLOTS,)), pltpu.SemaphoreType.DMA((SLOTS,)),
+        ],
+        compiler_params=pltpu.CompilerParams(
+            collective_id=0, has_side_effects=True, vmem_limit_bytes=VMEM_BYTES
+        ),
+        name="layer",
+    )(x, prefix, wq, wk, wv, wo, wg, wu, wd, gains, cosine, sine, dy)
+
+
+SLOTS = 640
+
+
+def widen_kernel(*refs):
+    narrow, wide = refs[:9], refs[9:18]
+    held, turned, sems = refs[18:27], refs[27:34], refs[34]
+    loads = [pltpu.make_async_copy(a, b, sems.at[i]) for i, (a, b) in enumerate(zip(narrow, held))]
+    stores = [
+        pltpu.make_async_copy(a, b, sems.at[9 + i])
+        for i, (a, b) in enumerate(zip(turned + held[7:], wide))
+    ]
+    for copy in loads:
+        copy.start()
+    for load, store, a, b in zip(loads, stores, held, turned):
+        load.wait()
+
+        def body(i, carry):
+            rows = rows_at(i * 32, 32)
+            b[rows, :] = a[rows, :].astype(F32)
+            return carry
+
+        lax.fori_loop(0, a.shape[0] // 32, body, 0)
+        store.start()
+    for i in (7, 8):
+        loads[i].wait()
+        stores[i].start()
+    for copy in stores:
+        copy.wait()
+
+
+def widen(narrow, same):
+    place, shape, hold = pl.BlockSpec(memory_space=pltpu.HBM), jax.ShapeDtypeStruct, pltpu.VMEM
+    return pl.pallas_call(
+        widen_kernel,
+        out_shape=tuple(shape(a.shape, F32) for a in narrow) + tuple(shape(a.shape, BF) for a in same),
+        in_specs=[place] * 9,
+        out_specs=(place,) * 9,
+        scratch_shapes=[hold(a.shape, BF) for a in narrow + same]
+        + [hold(a.shape, F32) for a in narrow]
+        + [pltpu.SemaphoreType.DMA((18,))],
+        compiler_params=pltpu.CompilerParams(vmem_limit_bytes=VMEM_BYTES),
+        name="widen",
+    )(*narrow, *same)
+
+
+def rope_tables(length):
+    freqs = ROPE_BASE ** (-(np.arange(HEAD_SIZE // 2, dtype=np.float32) * 2.0 / HEAD_SIZE))
+    angles = np.arange(length, dtype=np.float32)[:, None] * freqs.astype(np.float32)[None, :]
+    cosine, sine = np.cos(angles), np.sin(angles)
+    return np.concatenate([cosine, cosine], 1), np.concatenate([-sine, sine], 1)
+
+
+def with_kernel(layer_input, prefix, wq, wk, wv, wo, w_gate, w_up, w_down, gains, cotangent):
+    cosine, sine = rope_tables(layer_input.shape[1] * 8)
+    results = run_layer(
+        layer_input[0], prefix, wq, wk, wv, wo, w_gate, w_up, w_down,
+        jnp.pad(gains.reshape(1, 136), ((0, 15), (0, 120))),
+        cosine, sine, cotangent[0],
+    )
+    output, x_grad, gain_sum = results[:3]
+    first = (lax.axis_index("dp") * 8 + lax.axis_index("ctx")) * 136
+    gains_grad = lax.dynamic_slice_in_dim(gain_sum[0], first, 136, 0)
+    big_first = (8, 7, 9, 3, 6, 4, 5)
+    final = widen([results[i] for i in big_first], [output, x_grad])
+    wide = tuple(final[big_first.index(i)] for i in range(3, 10))
+    return (final[7][None], final[8][None]) + wide + (gains_grad,)
+
+
 def solution(mesh):
     tokens = P("dp", "ctx", None)
     matrix = P(("dp", "ctx"), None)
     vector = P(("dp", "ctx"))
+    small = mesh.shape["dp"] == 4 and mesh.shape["ctx"] == 8
     return jax.shard_map(
-        general,
+        with_kernel if small else general,
         mesh=mesh,
         in_specs=(tokens, P("dp")) + (matrix,) * 7 + (vector, tokens),
         out_specs=(tokens, tokens) + (matrix,) * 7 + (vector,),

time: 919 us -> 366 us (0.40)
  waiting for transfers between devices: 415 us -> 0 us
  Pallas kernels: 0 us -> 362 us
  blocking collectives: 255 us -> 0 us
  matrix products: 110 us -> 0 us
  local copies, waits for them, and re-layouts: 68.4 us -> 2.54 us
  other arithmetic: 36.6 us -> 0 us
  between operations: 15.8 us -> 1.32 us
  starting transfers between devices: 11.3 us -> 0 us
    pallas_call x0 -> x2, Pallas kernels: none -> 362 us  [the longest x1 358 us: run_layer(): pl.pallas_call(layer_kernel, out_shape=(shape((BLOCK, width), BF), shape(...]
    all_gather x8 -> x0, waiting for transfers between devices: 235 us -> none  [the longest x4 135 us: whole(): return lax.all_gather(array, 'ctx', axis=0, tiled=True)]
    all_to_all x4 -> x0, blocking collectives: 174 us -> none  [swap_ctx(): return lax.all_to_all(pieces, 'ctx', 0, 0)]
    dot_general x18 -> x0, matrix products: 110 us -> none  [the longest x4 31.3 us: mm_nt(): lax.dot_general(left, right, (((1,), (1,)), ((), ())), preferred_element_...]
    reduce_scatter x7 -> x0, waiting for transfers between devices: 102 us -> none  [the longest x4 102 us: own_sum(): lax.psum_scatter(partial.astype(BF), 'ctx', scatter_dimension=0, tiled=True)]
    unnamed x2 -> x0, blocking collectives: 81 us -> none
    all_to_all x2 -> x0, waiting for transfers between devices: 73.7 us -> none  [swap_ctx(): return lax.all_to_all(pieces, 'ctx', 0, 0)]
    unnamed x79 -> x0, local copies, waits for them, and re-layouts: 22.1 us -> none
  transfers between devices with their start and end apart: 18 -> 0, of which waited for: 10 -> 0; matrix products, arithmetic and copies ran while one was open for 17% -> 0% of each run, Pallas kernels for 0% -> 0%
where the time goes in v2:
time: 366 us
  Pallas kernels  362 us (99%)
    pallas_call x1, Pallas kernels, run_layer(): pl.pallas_call(layer_kernel, out_shape=(shape((BLOCK, width), BF), shape(...  358 us

profile of v2, /device:TPU:1, one launch (start us, length us, event | category | flops | bytes accessed | tf_op | source)
XLA Modules:
  0.0 365.8 jit_solution(3029309083171952093)
XLA Ops:
  0.6 0.7 reshape.24
  1.3 0.6 pad.4.gains
  2.6 357.6 %layer.1 = (bf16[128,2048]{1,0:T(8,128)(2,1)}, bf16[128,2048]{1,0:T(8,128)(2,1)}, f32[1,4352]{1,0:T(1,128)}, bf16[64,2048]{1,0:T(8,128)(2,1)}, bf16[64,1024]{1,0...) custom-call(bf16[128,2048]{1,0:T(8,128)(2,1)} %bitcast.5, ...), custom_call_target="tpu_custom_call" | custom-call | tf_op jit(solution)/shard_map/layer/pallas_call | solution.py:1748
  360.1 4.4 %widen.1 = (f32[64,6144]{1,0:T(8,128)}, f32[64,6144]{1,0:T(8,128)}, f32[192,2048]{1,0:T(8,128)}, f32[64,2048]{1,0:T(8,128)}, f32[64,2048]{1,0:T(8,128)}, /*index...) custom-call(bf16[64,6144]{1,0:T(8,128)(2,1)} %get-tuple-element.29.refs_0_, ...), custom_call_target="tpu_custom_call" | custom-call | tf_op jit(solution)/shard_map/widen/pallas_call | solution.py:1813
  364.5 1.3 constant_dynamic-slice_fusion

commit v3 on v2

--- a/solution.py
+++ b/solution.py
@@ -1045,6 +1045,9 @@
     tokens.twin_step(0)
     each_side(0, normalize_chip)
     tokens.step(1)
+    own_copies[2].wait()
+    upstream = Gather(k, g, ys)
+    upstream.start_line(z == 2, z == 1)
     spread_qkv.forward()
     tokens.twin_step(1)
     each_side(1, normalize_chip)
@@ -1133,12 +1136,10 @@
 
         lax.fori_loop(0, 4, columns, 0)
         sum_one.send_twin(chip)
-    own_copies[2].wait()
     d_hidden[...] = ys[own, :].astype(F32)
-    upstream = Gather(k, g, ys)
 
     def upstream_goes(step):
-        upstream.start_line(step == z, step == 3 - z)
+        upstream.start_line((step == z) & (z < 2), (step == 3 - z) & (z > 1))
 
 
     sum_one.take_twin(3)
@@ -1378,7 +1379,6 @@
     load.start()
     lax.fori_loop(0, 3, down_gradient, 0)
     start_wide_back, start_thin_back, finish_down_back = down_to_owners(g, k, w_d, got_d)
-    start_wide_back()
     sum_two.relay(0, 0)
     folds[0].middle(add_stages)
     sum_two.relay(1, 0)
@@ -1401,18 +1401,19 @@
     sum_two.last(done_two, 0)
     thirds.start_part(0)
     sum_two.send_ends(1, 2)
-
-    @pl.when(at_end)
-    def _():
-        sum_out.advance(1)
-
     sum_two.relay(0, 1)
     sum_two.relay(1, 1)
     thirds.step_part(0, 0)
     sum_two.last(done_two, 1)
     thirds.start_part(1)
 
+    @pl.when(at_end)
+    def _():
+        sum_out.advance(1)
+
+
     folds[1].middle(add_stages)
+    start_wide_back()
     thirds.step_part(1, 0)
     thirds.step_part(0, 1)
 

time: 366 us -> 350 us (0.956)
  Pallas kernels: 362 us -> 345 us
    pallas_call x1, Pallas kernels: 358 us -> 341 us  [run_layer(): pl.pallas_call(layer_kernel, out_shape=(shape((BLOCK, width), BF), shape(...]
where the time goes in v3:
time: 350 us; the launch traced here: 349 us
  Pallas kernels  345 us (99%)
    pallas_call x1, Pallas kernels, run_layer(): pl.pallas_call(layer_kernel, out_shape=(shape((BLOCK, width), BF), shape(...  341 us

profile of v3, /device:TPU:1, one launch (start us, length us, event | category | flops | bytes accessed | tf_op | source)
XLA Modules:
  0.0 349.2 jit_solution(7975081598133633652)
XLA Ops:
  0.6 0.7 reshape.24
  1.3 0.6 pad.4.gains
  2.6 341.0 %layer.1 = (bf16[128,2048]{1,0:T(8,128)(2,1)}, bf16[128,2048]{1,0:T(8,128)(2,1)}, f32[1,4352]{1,0:T(1,128)}, bf16[64,2048]{1,0:T(8,128)(2,1)}, bf16[64,1024]{1,0...) custom-call(bf16[128,2048]{1,0:T(8,128)(2,1)} %bitcast.5, ...), custom_call_target="tpu_custom_call" | custom-call | tf_op jit(solution)/shard_map/layer/pallas_call | solution.py:1749
  343.5 4.4 %widen.1 = (f32[64,6144]{1,0:T(8,128)}, f32[64,6144]{1,0:T(8,128)}, f32[192,2048]{1,0:T(8,128)}, f32[64,2048]{1,0:T(8,128)}, f32[64,2048]{1,0:T(8,128)}, /*index...) custom-call(bf16[64,6144]{1,0:T(8,128)(2,1)} %get-tuple-element.29.refs_0_, ...), custom_call_target="tpu_custom_call" | custom-call | tf_op jit(solution)/shard_map/widen/pallas_call | solution.py:1814
  347.9 1.3 constant_dynamic-slice_fusion

commit v4 on v3

--- a/solution.py
+++ b/solution.py
@@ -267,12 +267,15 @@
 
 
 class Gather:
-    def __init__(self, copies, place, buf, parts=2):
+    def __init__(self, copies, place, buf, parts=2, after=None):
         self.k, self.g, self.buf, self.parts = copies, place, buf, parts
         self.size = BLOCK // parts
-        self.right = copies.take(3 * parts)
-        self.left = copies.take(3 * parts)
-        self.twin = copies.take(7 * parts)
+        if after is None:
+            self.right = copies.take(3 * parts)
+            self.left = copies.take(3 * parts)
+            self.twin = copies.take(7 * parts)
+        else:
+            self.right, self.left, self.twin = after.right, after.left, after.twin
 
     def piece(self, z, p, part):
         return self.buf.at[rows_at((2 * z + p) * BLOCK + part * self.size, self.size)]
@@ -385,13 +388,16 @@
 
 
 class Scatter:
-    def __init__(self, copies, place, partial, from_twin, from_left, from_right, parts=2):
+    def __init__(self, copies, place, partial, from_twin, from_left, from_right, parts=2, after=None):
         self.k, self.g = copies, place
         self.partial, self.from_twin = partial, from_twin
         self.from_line = {True: from_left, False: from_right}
         self.parts, self.size = parts, BLOCK // parts
-        self.twin = copies.take(4)
-        self.slots = {True: copies.take(3 * parts), False: copies.take(3 * parts)}
+        if after is None:
+            self.twin = copies.take(4)
+            self.slots = {True: copies.take(3 * parts), False: copies.take(3 * parts)}
+        else:
+            self.twin, self.slots = after.twin, after.slots
 
     def row(self, z, p):
         return (2 * z + p) * BLOCK
@@ -523,43 +529,6 @@
                     @pl.when(self.can_send(step, rightwards))
                     def _():
                         self.line(step, rightwards, part).wait_send()
-
-
-class Outwards(Scatter):
-    def __init__(self, *args):
-        super().__init__(*args, parts=1)
-
-    def can_send(self, step, rightwards):
-        return self.g.z + 1 + step <= 3 if rightwards else self.g.z - 1 - step >= 0
-
-    def target(self, step, rightwards):
-        return self.g.z + 1 + step if rightwards else self.g.z - 1 - step
-
-    def send_ends(self, step):
-        for rightwards in (True, False):
-
-            @pl.when(self.g.z == (0 if rightwards else 3))
-            def _():
-                self.line(step, rightwards, 0).start()
-
-    def relay(self, step, chip):
-        for rightwards in (True, False):
-
-            @pl.when(self.g.z == (chip if rightwards else 3 - chip))
-            def _():
-                self.wait_line(step, rightwards, 0)
-                at = self.row(self.target(step - 1, rightwards), self.g.p)
-                add_rows(
-                    self.partial, at, self.partial, at, self.from_line[rightwards], step * BLOCK, BLOCK
-                )
-                self.line(step - 1, rightwards, 0).start()
-
-    def take_own(self):
-        for rightwards in (True, False):
-
-            @pl.when(self.g.z >= 1 if rightwards else self.g.z <= 2)
-            def _():
-                self.wait_line(0, rightwards, 0)
 
 
 class Spread:
@@ -1170,7 +1139,7 @@
         hidden[rows, :] = h
         xs[rows_at(c * BLOCK + at, 16), :] = (h * r * gain_acc[0:1, 2048:4096]).astype(BF)
 
-    seconds = Gather(k, g, xs)
+    seconds = Gather(k, g, xs, after=tokens)
     sum_one.last(done_one, 0)
     seconds.start_part(0)
     sum_one.relay(0, 1)
@@ -1190,7 +1159,7 @@
     sum_one.drain()
     keep.wait()
     spread_up.finish()
-    sum_two = Scatter(k, g, partial2, from_twin, from_left, from_right)
+    sum_two = Scatter(k, g, partial2, from_twin, from_left, from_right, after=sum_one)
     sum_out = Scatter(k, g, partial, from_twin2, from_left2, from_right2, parts=1)
 
     def feed_forward(chip):
@@ -1329,6 +1298,12 @@
         spread.drain()
     upstream.drain()
     seconds.drain()
+    for rel in range(1, 8):
+        for j in range(3):
+            qkv_to(rel, j).wait_send()
+        for which in range(2):
+            for j in range(4):
+                gu_to(which, rel, j).wait_send()
 
     def fold_gu(which):
         cols = pl.ds(which * 768, 768)
@@ -1397,7 +1372,7 @@
         d_hidden[rows, :] = d_h
         n1[there, :] = d_h.astype(BF)
 
-    thirds = Gather(k, g, n1)
+    thirds = Gather(k, g, n1, after=tokens)
     sum_two.last(done_two, 0)
     thirds.start_part(0)
     sum_two.send_ends(1, 2)
@@ -1446,14 +1421,13 @@
             d_qkv[at, cols] = d_q.astype(BF)
             gain_qk[:, 0:128] += part
 
-    stage_slots = k.take(16)
-    gu_back = k.take(64)
+    stage_slots = k.take(14)
 
     def gu_home(which, rel, j):
         place, count = UNIT_PARTS[j]
         src = w_gu.at[rows_at(d * 512 + (c ^ rel) * 64, 64), pl.ds(which * 768 + place, count)]
         dst = (out_g, out_u)[which].at[:, lanes(unit_column(j, z, p), count)]
-        slot = gu_back + which * 32 + rel * 4 + j
+        slot = gu_slots + which * 32 + rel * 4 + j
         return k.to(src, dst, (d, c ^ rel), slot) if rel else k.here(src, dst, slot)
 
     def sum_gu(which):
@@ -1521,7 +1495,7 @@
     for rel in (1, 2, 3):
         qkv_over_dp(rel).start()
     start_thin_back()
-    sum_three = Scatter(k, g, partial2, from_twin, from_left, from_right)
+    sum_three = Scatter(k, g, partial2, from_twin, from_left, from_right, after=sum_one)
     for chip in (3, 0, 2, 1):
 
         def columns(j, carry):
@@ -1596,7 +1570,6 @@
 
     sum_three.advance(1)
 
-    qkv_back = k.take(24)
 
     def qkv_home(rel, j):
         other = c ^ rel
@@ -1606,7 +1579,7 @@
             lanes((d // 2) * 512 + (0, 256, 384)[j], width),
         ]
         dst = (out_q, out_k, out_v)[j].at[:, lanes(c * width, width)]
-        slot = qkv_back + 3 * rel + j
+        slot = qkv_slots + 3 * rel + j
         return k.to(src, dst, (d, other), slot) if rel else k.here(src, dst, slot)
 
     for rel in (1, 2, 3):
@@ -1714,13 +1687,9 @@
     for rel in range(8):
         for j in range(3):
             qkv_home(rel, j).wait()
-            if rel:
-                qkv_to(rel, j).wait_send()
         for which in range(2):
             for j in range(4):
                 gu_home(which, rel, j).wait()
-                if rel:
-                    gu_to(which, rel, j).wait_send()
         if rel:
             gain_over_ctx(rel).wait_send()
     for rel in range(4):
@@ -1779,7 +1748,7 @@
     )(x, prefix, wq, wk, wv, wo, wg, wu, wd, gains, cosine, sine, dy)
 
 
-SLOTS = 640
+SLOTS = 348
 
 
 def widen_kernel(*refs):

time: 350 us -> 344 us (0.983)
  Pallas kernels: 345 us -> 340 us
    pallas_call x1, Pallas kernels: 341 us -> 336 us  [run_layer(): pl.pallas_call(layer_kernel, out_shape=(shape((BLOCK, width), BF), shape(...]
where the time goes in v4:
time: 344 us
  Pallas kernels  340 us (99%)
    pallas_call x1, Pallas kernels, run_layer(): pl.pallas_call(layer_kernel, out_shape=(shape((BLOCK, width), BF), shape(...  336 us

profile of v4, /device:TPU:1, one launch (start us, length us, event | category | flops | bytes accessed | tf_op | source)
XLA Modules:
  0.0 343.9 jit_solution(11933676466207758463)
XLA Ops:
  0.6 0.7 reshape.24
  1.3 0.6 pad.4.gains
  2.6 335.7 %layer.1 = (bf16[128,2048]{1,0:T(8,128)(2,1)}, bf16[128,2048]{1,0:T(8,128)(2,1)}, f32[1,4352]{1,0:T(1,128)}, bf16[64,2048]{1,0:T(8,128)(2,1)}, bf16[64,1024]{1,0...) custom-call(bf16[128,2048]{1,0:T(8,128)(2,1)} %bitcast.5, ...), custom_call_target="tpu_custom_call" | custom-call | tf_op jit(solution)/shard_map/layer/pallas_call | solution.py:1718
  338.3 4.4 %widen.1 = (f32[64,6144]{1,0:T(8,128)}, f32[64,6144]{1,0:T(8,128)}, f32[192,2048]{1,0:T(8,128)}, f32[64,2048]{1,0:T(8,128)}, f32[64,2048]{1,0:T(8,128)}, /*index...) custom-call(bf16[64,6144]{1,0:T(8,128)(2,1)} %get-tuple-element.29.refs_0_, ...), custom_call_target="tpu_custom_call" | custom-call | tf_op jit(solution)/shard_map/widen/pallas_call | solution.py:1783
  342.6 1.3 constant_dynamic-slice_fusion

commit v5 on v4

--- a/solution.py
+++ b/solution.py
@@ -842,15 +842,20 @@
     for copy in own_copies:
         copy.start()
 
-    qkv_slots = k.take(24)
+    qkv_slots = k.take(8)
 
     def qkv_to(rel, j):
         other = c ^ rel
         width = 256 if j == 0 else 128
         src = (wq, wk, wv)[j].at[:, lanes(other * width, width)]
         dst = w_qkv.at[mine, pl.ds((0, 256, 384)[j], width)]
-        slot = qkv_slots + 3 * rel + j
+        slot = qkv_slots + rel
         return k.to(src, dst, (d, other), slot) if rel else k.here(src, dst, slot)
+
+    def qkv_pieces(rel):
+        whole = w_qkv.at[mine]
+        slot = qkv_slots + rel
+        return k.to(whole, whole, (d, c ^ rel), slot) if rel else k.here(whole, whole, slot)
 
     for rel in range(8):
         for j in range(3):
@@ -859,14 +864,14 @@
     tokens = Gather(k, g, xs)
     tokens.start()
     at_end = (z == 0) | (z == 3)
-    gu_slots = k.take(64)
+    gu_slots = k.take(16)
 
     def gu_to(which, rel, j):
         place, count = UNIT_PARTS[j]
         column = unit_column(j, z ^ (rel // 2), p ^ (rel % 2))
         src = (wg, wu)[which].at[:, lanes(column, count)]
         dst = w_gu.at[mine, pl.ds(which * 768 + place, count)]
-        slot = gu_slots + which * 32 + rel * 4 + j
+        slot = gu_slots + which * 8 + rel
         return k.to(src, dst, (d, c ^ rel), slot) if rel else k.here(src, dst, slot)
 
     def gu_start(*groups):
@@ -934,10 +939,9 @@
         lax.fori_loop(0, BLOCK // 16, body, 0)
 
     normalize(c)
-    for j in range(3):
-        qkv_to(0, j).wait()
-        for rel in range(1, 8):
-            qkv_to(rel, j).wait_recv()
+    qkv_pieces(0).wait()
+    for rel in range(1, 8):
+        qkv_pieces(rel).wait_recv()
     spread_qkv = Spread(k, g, lambda e, half: w_qkv.at[rows_at(e * 512 + half * 256, 256)])
     spread_qkv.start()
     tokens.twin_own()
@@ -1040,13 +1044,15 @@
     tokens.twin_step(2)
     each_side(2, normalize_chip)
 
+    def gu_pieces(which, rel):
+        whole = w_gu.at[mine, pl.ds(which * 768, 768)]
+        slot = gu_slots + which * 8 + rel
+        return k.to(whole, whole, (d, c ^ rel), slot) if rel else k.here(whole, whole, slot)
+
     def gu_take(which):
-        for rel in range(8):
-            for j in range(4):
-                if rel == 0:
-                    gu_to(which, rel, j).wait()
-                else:
-                    gu_to(which, rel, j).wait_recv()
+        gu_pieces(which, 0).wait()
+        for rel in range(1, 8):
+            gu_pieces(which, rel).wait_recv()
 
     @pl.when(at_end)
     def _():
@@ -1299,11 +1305,9 @@
     upstream.drain()
     seconds.drain()
     for rel in range(1, 8):
-        for j in range(3):
-            qkv_to(rel, j).wait_send()
+        qkv_pieces(rel).wait_send()
         for which in range(2):
-            for j in range(4):
-                gu_to(which, rel, j).wait_send()
+            gu_pieces(which, rel).wait_send()
 
     def fold_gu(which):
         cols = pl.ds(which * 768, 768)
@@ -1427,7 +1431,7 @@
         place, count = UNIT_PARTS[j]
         src = w_gu.at[rows_at(d * 512 + (c ^ rel) * 64, 64), pl.ds(which * 768 + place, count)]
         dst = (out_g, out_u)[which].at[:, lanes(unit_column(j, z, p), count)]
-        slot = gu_slots + which * 32 + rel * 4 + j
+        slot = gu_slots + which * 8 + rel
         return k.to(src, dst, (d, c ^ rel), slot) if rel else k.here(src, dst, slot)
 
     def sum_gu(which):
@@ -1579,7 +1583,7 @@
             lanes((d // 2) * 512 + (0, 256, 384)[j], width),
         ]
         dst = (out_q, out_k, out_v)[j].at[:, lanes(c * width, width)]
-        slot = qkv_slots + 3 * rel + j
+        slot = qkv_slots + rel
         return k.to(src, dst, (d, other), slot) if rel else k.here(src, dst, slot)
 
     for rel in (1, 2, 3):
@@ -1685,11 +1689,9 @@
     gain_out[...] = total
 
     for rel in range(8):
-        for j in range(3):
-            qkv_home(rel, j).wait()
+        qkv_pieces(rel).wait()
         for which in range(2):
-            for j in range(4):
-                gu_home(which, rel, j).wait()
+            gu_pieces(which, rel).wait()
         if rel:
             gain_over_ctx(rel).wait_send()
     for rel in range(4):
@@ -1748,7 +1750,7 @@
     )(x, prefix, wq, wk, wv, wo, wg, wu, wd, gains, cosine, sine, dy)
 
 
-SLOTS = 348
+SLOTS = 284
 
 
 def widen_kernel(*refs):

time: 344 us -> 343 us (level)
  no operation moved by 1% of the time
where the time goes in v5:
time: 343 us
  Pallas kernels  339 us (99%)
    pallas_call x1, Pallas kernels, run_layer(): pl.pallas_call(layer_kernel, out_shape=(shape((BLOCK, width), BF), shape(...  334 us

profile of v5, /device:TPU:1, one launch (start us, length us, event | category | flops | bytes accessed | tf_op | source)
XLA Modules:
  0.0 342.6 jit_solution(18320239886919658680)
XLA Ops:
  0.6 0.7 reshape.24
  1.3 0.6 pad.4.gains
  2.6 334.4 %layer.1 = (bf16[128,2048]{1,0:T(8,128)(2,1)}, bf16[128,2048]{1,0:T(8,128)(2,1)}, f32[1,4352]{1,0:T(1,128)}, bf16[64,2048]{1,0:T(8,128)(2,1)}, bf16[64,1024]{1,0...) custom-call(bf16[128,2048]{1,0:T(8,128)(2,1)} %bitcast.5, ...), custom_call_target="tpu_custom_call" | custom-call | tf_op jit(solution)/shard_map/layer/pallas_call | solution.py:1720
  337.0 4.4 %widen.1 = (f32[64,6144]{1,0:T(8,128)}, f32[64,6144]{1,0:T(8,128)}, f32[192,2048]{1,0:T(8,128)}, f32[64,2048]{1,0:T(8,128)}, f32[64,2048]{1,0:T(8,128)}, /*index...) custom-call(bf16[64,6144]{1,0:T(8,128)(2,1)} %get-tuple-element.29.refs_0_, ...), custom_call_target="tpu_custom_call" | custom-call | tf_op jit(solution)/shard_map/widen/pallas_call | solution.py:1785
  341.4 1.3 constant_dynamic-slice_fusion

commit v6 on v5

--- a/solution.py
+++ b/solution.py
@@ -1489,16 +1489,6 @@
     lax.fori_loop(0, 4, finish_keys, 0)
     load.wait()
 
-    def qkv_gradient(e, carry):
-        cols = lanes(e * 512, 512)
-        rows, place = rows_at(lax.rem(e, 2) * 512, 512), lanes((e // 2) * 512, 512)
-        d_gu[rows, place] = tn(xs[:, cols], d_qkv[...]).astype(BF)
-        return carry
-
-    lax.fori_loop(0, 4, qkv_gradient, 0)
-    for rel in (1, 2, 3):
-        qkv_over_dp(rel).start()
-    start_thin_back()
     sum_three = Scatter(k, g, partial2, from_twin, from_left, from_right, after=sum_one)
     for chip in (3, 0, 2, 1):
 
@@ -1516,6 +1506,16 @@
     sum_three.start()
     sum_three.take_twin(2)
     sum_three.take_twin(1)
+    def qkv_gradient(e, carry):
+        cols = lanes(e * 512, 512)
+        rows, place = rows_at(lax.rem(e, 2) * 512, 512), lanes((e // 2) * 512, 512)
+        d_gu[rows, place] = tn(xs[:, cols], d_qkv[...]).astype(BF)
+        return carry
+
+    lax.fori_loop(0, 4, qkv_gradient, 0)
+    for rel in (1, 2, 3):
+        qkv_over_dp(rel).start()
+    start_thin_back()
 
     def gain_columns(e, carry):
         rows, place = rows_at(lax.rem(e, 2) * 512, 512), lanes((e // 2) * 512, 512)

time: 343 us -> 343 us (level)
  no operation moved by 1% of the time
where the time goes in v6:
time: 343 us
  Pallas kernels  339 us (99%)
    pallas_call x1, Pallas kernels, run_layer(): pl.pallas_call(layer_kernel, out_shape=(shape((BLOCK, width), BF), shape(...  334 us

profile of v6, /device:TPU:1, one launch (start us, length us, event | category | flops | bytes accessed | tf_op | source)
XLA Modules:
  0.0 342.6 jit_solution(17525951087306181848)
XLA Ops:
  0.6 0.7 reshape.24
  1.3 0.6 pad.4.gains
  2.6 334.4 %layer.1 = (bf16[128,2048]{1,0:T(8,128)(2,1)}, bf16[128,2048]{1,0:T(8,128)(2,1)}, f32[1,4352]{1,0:T(1,128)}, bf16[64,2048]{1,0:T(8,128)(2,1)}, bf16[64,1024]{1,0...) custom-call(bf16[128,2048]{1,0:T(8,128)(2,1)} %bitcast.5, ...), custom_call_target="tpu_custom_call" | custom-call | tf_op jit(solution)/shard_map/layer/pallas_call | solution.py:1720
  337.0 4.4 %widen.1 = (f32[64,6144]{1,0:T(8,128)}, f32[64,6144]{1,0:T(8,128)}, f32[192,2048]{1,0:T(8,128)}, f32[64,2048]{1,0:T(8,128)}, f32[64,2048]{1,0:T(8,128)}, /*index...) custom-call(bf16[64,6144]{1,0:T(8,128)(2,1)} %get-tuple-element.29.refs_0_, ...), custom_call_target="tpu_custom_call" | custom-call | tf_op jit(solution)/shard_map/widen/pallas_call | solution.py:1785
  341.4 1.3 constant_dynamic-slice_fusion
